TPU v7x, 512 devices: a whole 4x4x16 slice. The times are simulated.
512 devices in a mesh: replica: 32 (over z_hi, x, core), fsdp: 16 (over y, z_lo).
Axes of the slice: x: 4, y: 4, z: 16 (z_hi: 4, z_lo: 4; z = z_hi * 4 + z_lo), core: 2. Of those that a mesh axis runs over, the one named last changes fastest.
Arguments:
- activations: bfloat16 [32, 1, 2048, 4096], P('replica', None, 'fsdp'), may hold values from -6 to 6
- cotangent: bfloat16 [32, 1, 2048, 512], P('replica', None, 'fsdp'), may hold values from -6 to 6
- params: float32 [32, 4096, 512], P('replica', 'fsdp'), may hold values from -6 to 6
- first_moment: bfloat16 [32, 4096, 512], P('replica', 'fsdp'), may hold values from -3 to 3
- second_moment: float32 [32, 4096, 512], P('replica', 'fsdp'), may hold values from 0.01 to 1
- anchor: bfloat16 [4096, 512], P('fsdp'), may hold values from -6 to 6
- outer_momentum: bfloat16 [4096, 512], P('fsdp'), may hold values from -2 to 2
Outputs:
- merged: float32 [32, 4096, 512], P('replica', 'fsdp')
- new_first_moment: float32 [32, 4096, 512], P('replica', 'fsdp')
- input_grad: bfloat16 [32, 1, 2048, 4096], P('replica', None, 'fsdp')
All inputs are finite; a program needn't handle non-finite values.
Results may differ from a plain program's by a relative error of at most 0.0049.
Values may be sent and summed in bfloat16 or wider, within the bound.
A program may use at most 64 MiB of HBM per device.

v0:
```python
import jax
import jax.numpy as jnp
from jax import lax
from jax.sharding import PartitionSpec as P

D = 4096


BETA_FIRST = 0.9
BETA_SECOND = 0.95
EPSILON = 1e-08
WEIGHT_DECAY = 0.1
INNER_RATE = 0.03
OUTER_RATE = 0.7
OUTER_MOMENT = 0.9
MIXING = 0.5


def on_device(activations, cotangent, params, first_moment, second_moment, anchor, outer_momentum):
    factor = float(D) ** (-0.5)
    local_rows = activations[0]
    local_upstream = cotangent[0]
    columns = lax.all_to_all(local_rows, "fsdp", split_axis=2, concat_axis=1, tiled=True)
    all_upstream = lax.all_gather(local_upstream, "fsdp", axis=1, tiled=True)
    gradients = (
        jnp.einsum("std,stk->sdk", columns, all_upstream, preferred_element_type=jnp.float32)
        * factor
    )
    global_old = anchor.astype(jnp.float32)
    outer_delta = global_old - params[0]
    momentum = outer_momentum.astype(jnp.float32)
    replicas = lax.axis_size("replica")
    outer_grad = lax.psum(outer_delta, "replica") / replicas
    moment_new = OUTER_MOMENT * momentum + outer_grad
    global_new = global_old - OUTER_RATE * (outer_grad + OUTER_MOMENT * moment_new)
    weights = params[0]
    first_state = first_moment[0].astype(jnp.float32)
    second = second_moment[0]
    scaled = (weights * factor).astype(jnp.bfloat16)
    upstream_now = local_upstream[0]
    gathered = jnp.dot(
        upstream_now,
        lax.all_gather(scaled, "fsdp", axis=0, tiled=True).T,
        preferred_element_type=jnp.float32,
    )
    outputs = [gathered.astype(jnp.bfloat16)]
    gradient = gradients[0]
    first_state = BETA_FIRST * first_state + (1.0 - BETA_FIRST) * gradient
    second = BETA_SECOND * second + (1.0 - BETA_SECOND) * gradient * gradient
    weights = weights - INNER_RATE * (
        first_state / (jnp.sqrt(second) + EPSILON) + WEIGHT_DECAY * weights
    )
    merged = MIXING * weights + (1.0 - MIXING) * global_new
    return (merged[None], first_state[None], jnp.stack(outputs)[None])


def solution(mesh):
    placed = (
        P("replica", None, "fsdp", None),
        P("replica", None, "fsdp", None),
        P("replica", "fsdp", None),
        P("replica", "fsdp", None),
        P("replica", "fsdp", None),
        P("fsdp", None),
        P("fsdp", None),
    )
    return jax.shard_map(
        on_device,
        mesh=mesh,
        in_specs=placed,
        out_specs=(
            P("replica", "fsdp", None),
            P("replica", "fsdp", None),
            P("replica", None, "fsdp", None),
        ),
        check_vma=False,
    )
```

profile of v0, /device:TPU:1, one launch (start us, length us, event | category | flops | bytes accessed | tf_op | source)
XLA Modules:
  0.0 436.1 jit_solution(941855968150211018)
XLA Ops:
  8.0 0.0 copy-start.1
  8.0 0.0 all-gather.6.cloned.1.call-start
  8.1 0.7 all-gather.6.cloned.1.call-update
  8.7 0.0 all-reduce.2.cloned.1.call-start
  8.8 2.1 fusion.12
  10.9 0.0 all-reduce.2.cloned.1.call-update
  10.9 0.0 all-gather.4.cloned.1.call-start
  11.0 0.7 all-gather.4.cloned.1.call-update
  11.7 0.0 copy-done.1
  11.7 2.8 copy.18
  14.5 0.5 broadcast.32
  15.0 22.4 %reduce = bf16[4096,128]{1,0:T(8,128)(2,1)S(1)} reduce(bf16[4096,1,128]{2,1,0:T(2,128)(2,1)S(1)} %bitcast.55, bf16[]{:T(256)} %broadcast.32), dimensions={1}, to_apply=%bitcast.48.reduce_sub_computation | reduce | bytes 2097154
  37.4 0.3 reshape.26
  37.7 62.7 %all_to_all.15 = bf16[16,2,16384]{2,1,0:T(2,128)(2,1)S(1)} all-to-all(bf16[16,2,16384]{2,1,0:T(2,128)(2,1)S(1)} %reshape.26), channel_id=1, replica_groups=mesh['replica'=32,'fsdp'=16] {'fsdp'}, dimensions={0} | all-to-all | bytes 2097152 | tf_op jit(solution)/shard_map/all_to_all | solution.py:23
  100.4 1.0 reshape.27
  101.5 0.0 copy-start.6
  101.5 0.1 copy.21
  101.7 0.5 copy.19
  102.2 7.6 %all-gather.6.cloned.1.call-done = bf16[1,1,2048,512]{3,2,1,0:T(8,128)(2,1)} async-done(((bf16[1,1,128,512]{3,2,1,0:T(8,128)(2,1)}), bf16[1,1,2048,512]{3,2,1,0:T(8,128)(2,1)}) %all-gather.6.cloned.1.call-update) | async-done | bytes 2097168 | tf_op jit(solution)/shard_map/all_gather | solution.py:24
  109.8 0.0 copy-done.6
  109.8 0.0 copy-start
  109.8 0.0 copy-start.2
  109.8 0.0 copy-start.4
  109.8 0.0 copy-start.5
  109.9 3.2 bitcast_add_fusion
  113.1 0.0 copy-start.3
  113.1 308.4 %all-reduce.2.cloned.1.call-done = f32[256,512]{1,0:T(8,128)} async-done(((f32[256,512]{1,0:T(8,128)}), f32[256,512]{1,0:T(8,128)}) %all-reduce.2.cloned.1.call-update) | async-done | bytes 524304 | tf_op jit(solution)/shard_map/psum | solution.py:33
  421.5 0.0 copy-done
  421.5 0.0 copy-done.2
  421.5 0.0 copy-done.4
  421.5 0.0 copy-done.5
  421.5 2.4 fusion.5
  423.9 0.0 all-gather.4.cloned.1.call-done
  423.9 0.0 copy-done.3
  423.9 3.4 fusion
  427.4 1.3 copy.20
Async XLA Ops:
  8.0 3.7 copy-start.1
  8.0 101.8 %all-gather.6.cloned.1.call-start = ((), (), s32[]{:S(2)}) async-start(), calls=%async_computation.3 | async-start | bytes 2228224 | tf_op jit(solution)/shard_map/all_gather | solution.py:24
  8.7 412.8 %all-reduce.2.cloned.1.call-start = ((), (), s32[]{:S(2)}) async-start(), calls=%async_computation.1 | async-start | bytes 1048576 | tf_op jit(solution)/shard_map/psum | solution.py:33
  10.9 413.0 %all-gather.4.cloned.1.call-start = ((), (), s32[]{:S(2)}) async-start(), calls=%async_computation.2 | async-start | bytes 4456448 | tf_op jit(solution)/shard_map/all_gather | solution.py:43
  101.5 8.3 %copy-start.6 = (bf16[1,256,512]{2,1,0:T(8,128)(2,1)S(1)}, bf16[1,256,512]{2,1,0:T(8,128)(2,1)}, u32[]{:S(2)}) copy-start(bf16[1,256,512]{2,1,0:T(8,128)(2,1)} %param.10) | copy-start | bytes 786436
  109.8 311.7 %copy-start = (f32[1,256,512]{2,1,0:T(8,128)S(1)}, f32[1,256,512]{2,1,0:T(8,128)}, u32[]{:S(2)}) copy-start(f32[1,256,512]{2,1,0:T(8,128)} %param.9) | copy-start | bytes 1572868
  109.8 311.7 %copy-start.2 = (bf16[256,512]{1,0:T(8,128)(2,1)S(1)}, bf16[256,512]{1,0:T(8,128)(2,1)}, u32[]{:S(2)}) copy-start(bf16[256,512]{1,0:T(8,128)(2,1)} %param.12) | copy-start | bytes 786436
  109.8 311.7 %copy-start.4 = (f32[1,256,512]{2,1,0:T(8,128)S(1)}, f32[1,256,512]{2,1,0:T(8,128)}, u32[]{:S(2)}) copy-start(f32[1,256,512]{2,1,0:T(8,128)} %param.11) | copy-start | bytes 1572868
  109.8 311.7 %copy-start.5 = (bf16[256,512]{1,0:T(8,128)(2,1)S(1)}, bf16[256,512]{1,0:T(8,128)(2,1)}, u32[]{:S(2)}) copy-start(bf16[256,512]{1,0:T(8,128)(2,1)} %param.13) | copy-start | bytes 786436
  113.1 310.8 %copy-start.3 = (bf16[1,1,128,512]{3,2,1,0:T(8,128)(2,1)S(1)}, bf16[1,1,128,512]{3,2,1,0:T(8,128)(2,1)}, u32[]{:S(2)}) copy-start(bf16[1,1,128,512]{3,2,1,0:T(8,128)(2,1)} %param.8) | copy-start | bytes 393220
Sparse Core Ops, SparseCore 0:
  11.1 98.6 all-gather.5
  112.7 113.0 all-gather.3
Sparse Core Ops, SparseCore 1:
  12.7 408.8 all-reduce.1
where the time goes:
time: 436 us
  waiting for transfers between devices  317 us (73%)
  blocking collectives  62.7 us (14%)
  other arithmetic  26.9 us (6%)
  between operations  15.6 us (4%)
  local copies, waits for them, and re-layouts  6.68 us (2%)
  matrix products  6.68 us (2%)
    psum x1, waiting for transfers between devices, on_device(): outer_grad = lax.psum(outer_delta, 'replica') / replicas  308 us
    all_to_all x1, blocking collectives, on_device(): lax.all_to_all(local_rows, 'fsdp', split_axis=2, concat_axis=1, tiled=True)  62.7 us
    unnamed x1, other arithmetic  22.4 us
  transfers between devices with their start and end apart: 3, of which 2 were waited for; matrix products, arithmetic and copies ran while one was open for 8% of the time, Pallas kernels for 0%

commit v1 on v0

v1 whole, which is shorter than its diff:
```python
import jax
import jax.numpy as jnp
from jax import lax
from jax.experimental import pallas as pl
from jax.experimental.pallas import tpu as pltpu
from jax.sharding import PartitionSpec as P

D = 4096
KVW = 512
ROWS = 256
TOKENS = 128
RING = 4
LINE = 4
SPAN = ROWS * LINE
HALF = ROWS // 2
CHIPS = 8
CHUNK = ROWS // CHIPS
REPLICAS = 32

BETA_FIRST = 0.9
BETA_SECOND = 0.95
EPSILON = 1e-08
WEIGHT_DECAY = 0.1
INNER_RATE = 0.03
OUTER_RATE = 0.7
OUTER_MOMENT = 0.9
MIXING = 0.5

FACTOR = float(D) ** (-0.5)
MESH = pl.DeviceIdType.MESH
BF16 = jnp.bfloat16
F32 = jnp.float32


def kernel(
    act,
    cot,
    params,
    first,
    second,
    anchor,
    outer,
    merged_out,
    first_out,
    grad_out,
    acts,
    cots,
    scaled,
    partial,
    landed,
    relay,
    back,
    weights,
    firsts,
    seconds,
    anchors,
    outers,
    rounded,
    got_a,
    sum_a,
    sent_b,
    got_b,
    total,
    local_sem,
    cot_s,
    cot_r,
    act_s,
    act_r,
    w_s,
    w_r,
    part_s,
    part_r,
    back_s,
    back_r,
    a_s,
    a_r,
    b_s,
    b_r,
    d_s,
    d_r,
    out_sem,
):
    replica = lax.axis_index("replica")
    shard = lax.axis_index("fsdp")
    y, p = shard // LINE, shard % LINE
    group, m = replica // CHIPS, replica % CHIPS
    edge = (p == 0) | (p == LINE - 1)
    inner = (p == 1) | (p == 2)
    has_low, has_high = p > 0, p < LINE - 1
    upper = p // 2

    def mirrored(at):
        return at + upper * (LINE - 1 - 2 * at)

    is_end = 1 - (p + 1) % LINE // 2
    order = [mirrored(3), mirrored(2), mirrored(is_end), p]
    near = [p, mirrored(is_end), mirrored(2), mirrored(3)]
    ring = [lax.rem(y + j, RING) for j in range(RING)]
    chip = [lax.rem(m + j, CHIPS) for j in range(CHIPS)]
    swaps = [group + 1 - 2 * (group % 2), 3 - group]

    def on_ring(j):
        return {"fsdp": ring[j] * LINE + p}

    def on_line(at):
        return {"fsdp": y * LINE + at}

    def on_chip(j):
        return {"replica": group * CHIPS + chip[j]}

    def on_group(step):
        return {"replica": swaps[step] * CHIPS + m}

    def remote(src, dst, send, recv, where):
        return pltpu.make_async_remote_copy(
            src_ref=src,
            dst_ref=dst,
            send_sem=send,
            recv_sem=recv,
            device_id=where,
            device_id_type=MESH,
        )

    def rows_of(at, size):
        return pl.ds(pl.multiple_of(at * size, size), size)

    def features(ring_at, line_at):
        return pl.ds(pl.multiple_of(ring_at * SPAN + line_at * ROWS, ROWS), ROWS)

    own_rows = rows_of(y, TOKENS)
    loads = [
        pltpu.make_async_copy(params, weights, local_sem.at[0]),
        pltpu.make_async_copy(cot, cots.at[own_rows], local_sem.at[1]),
    ]
    for k in range(LINE):
        loads.append(
            pltpu.make_async_copy(
                act.at[:, features(y, order[k])], acts.at[k, own_rows], local_sem.at[2 + k]
            )
        )
    loads += [
        pltpu.make_async_copy(anchor, anchors, local_sem.at[6]),
        pltpu.make_async_copy(outer, outers, local_sem.at[7]),
        pltpu.make_async_copy(first, firsts, local_sem.at[8]),
        pltpu.make_async_copy(second, seconds, local_sem.at[9]),
    ]
    for load in loads:
        load.start()

    barrier = pltpu.get_barrier_semaphore()

    def greet(where):
        pl.semaphore_signal(barrier, inc=1, device_id=where, device_id_type=MESH)

    for step in range(2):
        greet(on_group(step))
    for j in range(1, CHIPS):
        greet(on_chip(j))
    for j in range(1, RING):
        greet(on_ring(j))

    @pl.when(has_low)
    def _():
        greet(on_line(p - 1))

    @pl.when(has_high)
    def _():
        greet(on_line(p + 1))

    with jax.named_scope("scale"):
        loads[0].wait()
        scaled[p] = (weights[...] * FACTOR).astype(BF16)
        rounded[...] = weights[...].astype(BF16)

    with jax.named_scope("barrier"):
        met = 2 + (CHIPS - 1) + (RING - 1)
        pl.semaphore_wait(barrier, met + 2 - is_end)

    cot_copies = [
        remote(cot, cots.at[own_rows], cot_s.at[j], cot_r.at[j], on_ring(j))
        for j in range(1, RING)
    ]
    act_copies = [
        [
            remote(
                act.at[:, features(ring[j], order[k])],
                acts.at[k, own_rows],
                act_s.at[k, j],
                act_r.at[k, j],
                on_ring(j),
            )
            for j in range(1, RING)
        ]
        for k in range(LINE)
    ]
    a_copies = [
        remote(
            rounded.at[rows_of(chip[j], CHUNK)],
            got_a.at[j],
            a_s.at[j],
            a_r.at[j],
            on_chip(j),
        )
        for j in range(1, CHIPS)
    ]
    b_copies = [
        remote(sent_b.at[step], got_b.at[step], b_s.at[step], b_r.at[step], on_group(step))
        for step in range(2)
    ]
    d_copies = [
        remote(total.at[m], total.at[m], d_s.at[j], d_r.at[j], on_chip(j))
        for j in range(1, CHIPS)
    ]

    def d_arrival(j):
        origin = lax.rem(m - j + CHIPS, CHIPS)
        return remote(total.at[origin], total.at[origin], d_s.at[j], d_r.at[j], on_chip(j))

    def w_copy(block, half, way, to):
        rows = scaled.at[block, pl.ds(half * HALF, HALF)]
        return remote(rows, rows, w_s.at[way, block, half], w_r.at[block, half], on_line(to))

    def part_copy(k, half, way, to):
        rows = pl.ds(half * HALF, HALF)
        return remote(
            relay.at[k, rows],
            landed.at[way, order[k], rows],
            part_s.at[k, half],
            part_r.at[way, order[k], half],
            on_line(to),
        )

    def part_arrival(way, block, half):
        rows = landed.at[way, block, pl.ds(half * HALF, HALF)]
        return remote(rows, rows, part_s.at[0, half], part_r.at[way, block, half], on_line(p))

    def back_copy(i, j):
        return remote(
            back.at[i, rows_of(ring[j], TOKENS)],
            grad_out.at[:, features(y, near[i])],
            back_s.at[i, j],
            back_r.at[i, j],
            on_ring(j),
        )

    def back_own(i):
        return pltpu.make_async_copy(
            back.at[i, own_rows], grad_out.at[:, features(y, near[i])], out_sem.at[i]
        )

    for copy in a_copies + cot_copies:
        copy.start()
    for half in range(2):

        @pl.when(has_low)
        def _():
            w_copy(p, half, 1, p - 1).start()

        @pl.when(has_high)
        def _():
            w_copy(p, half, 0, p + 1).start()

    for copies in act_copies:
        for copy in copies:
            copy.start()

    def pass_near(half):
        @pl.when(inner)
        def _():
            w_copy(p - 1, half, 0, p + 1).wait_recv()
            w_copy(p - 1, half, 0, p + 1).start()
            w_copy(p + 1, half, 1, p - 1).wait_recv()
            w_copy(p + 1, half, 1, p - 1).start()

    def pass_far(half):
        @pl.when(p == 1)
        def _():
            w_copy(3, half, 1, 0).wait_recv()
            w_copy(3, half, 1, 0).start()

        @pl.when(p == 2)
        def _():
            w_copy(0, half, 0, 3).wait_recv()
            w_copy(0, half, 0, 3).start()

    def at_end_wait(block):
        @pl.when(edge)
        def _():
            for half in range(2):
                w_copy(block, half, 0, p).wait_recv()

    def input_grad(i):
        back[i] = lax.dot_general(
            cots[...],
            scaled[near[i]],
            (((1,), (1,)), ((), ())),
            preferred_element_type=F32,
        ).astype(BF16)
        for j in range(1, RING):
            back_copy(i, j).start()
        back_own(i).start()

    def gradient(k):
        for copy in act_copies[k]:
            copy.wait_recv()
        loads[2 + k].wait()
        with jax.named_scope("product"):
            partial[k] = lax.dot_general(
                acts[k], cots[...], (((0,), (0,)), ((), ())), preferred_element_type=F32
            )
        if k == LINE - 1:
            return

        @pl.when(edge)
        def _():
            relay[k] = partial[k].astype(BF16)

        @pl.when(p == 0)
        def _():
            for half in range(2):
                part_copy(k, half, 0, 1).start()

        @pl.when(p == LINE - 1)
        def _():
            for half in range(2):
                part_copy(k, half, 1, LINE - 2).start()

    def pass_part(k, half):
        rows = pl.ds(half * HALF, HALF)

        @pl.when(inner)
        def _():
            goes_up = order[k] > p

            @pl.when(goes_up)
            def _():
                part_arrival(0, order[k], half).wait_recv()
                both = partial[k, rows] + landed[0, order[k], rows].astype(F32)
                relay[k, rows] = both.astype(BF16)
                part_copy(k, half, 0, p + 1).start()

            @pl.when(order[k] < p)
            def _():
                part_arrival(1, order[k], half).wait_recv()
                both = partial[k, rows] + landed[1, order[k], rows].astype(F32)
                relay[k, rows] = both.astype(BF16)
                part_copy(k, half, 1, p - 1).start()

    with jax.named_scope("pass_near0"):
        pass_near(0)
    with jax.named_scope("sum_a"):
        own_sum = weights[rows_of(m, CHUNK)]
        for j in range(1, CHIPS):
            a_copies[j - 1].wait_recv()
            own_sum += got_a[j].astype(F32)
        sum_a[...] = own_sum
        sent_b[0] = own_sum.astype(BF16)
        b_copies[0].start()
    with jax.named_scope("pass_near1"):
        pass_near(1)
    with jax.named_scope("cot"):
        loads[1].wait()
        for copy in cot_copies:
            copy.wait_recv()
    with jax.named_scope("ig0"):
        input_grad(0)
    with jax.named_scope("pass_far0"):
        pass_far(0)
    with jax.named_scope("grad0"):
        gradient(0)
    with jax.named_scope("sum_b0"):
        b_copies[0].wait_recv()
        sum_a[...] += got_b[0].astype(F32)
        sent_b[1] = sum_a[...].astype(BF16)
        b_copies[1].start()
    with jax.named_scope("pass_far1"):
        pass_far(1)
    with jax.named_scope("grad1"):
        gradient(1)
    with jax.named_scope("ig1"):
        at_end_wait(near[1])
        input_grad(1)
    with jax.named_scope("part0"):
        pass_part(0, 0)
        pass_part(0, 1)
    with jax.named_scope("grad2"):
        gradient(2)
    with jax.named_scope("sum_b1"):
        b_copies[1].wait_recv()
        sum_a[...] += got_b[1].astype(F32)
        total[m] = sum_a[...].astype(BF16)
        for copy in d_copies:
            copy.start()
    with jax.named_scope("ig2"):
        at_end_wait(near[2])
        input_grad(2)
    with jax.named_scope("grad3"):
        gradient(3)
    with jax.named_scope("part1"):
        pass_part(1, 0)
        pass_part(1, 1)
    with jax.named_scope("ig3"):
        at_end_wait(near[3])
        input_grad(3)
    with jax.named_scope("part2"):
        pass_part(2, 0)
        pass_part(2, 1)
    with jax.named_scope("outer"):
        for j in range(1, CHIPS):
            d_arrival(j).wait_recv()
        for load in loads[6:]:
            load.wait()
        mean = total[...].astype(F32).reshape(ROWS, KVW) * (1.0 / REPLICAS)
        old = anchors[...].astype(F32)
        outer_grad = old - mean
        moment = OUTER_MOMENT * outers[...].astype(F32) + outer_grad
        new = old - OUTER_RATE * (outer_grad + OUTER_MOMENT * moment)
        kept = MIXING * (1.0 - INNER_RATE * WEIGHT_DECAY)
        partial[0] = kept * weights[...] + (1.0 - MIXING) * new

    stores = []
    for half in range(2):
        rows = pl.ds(half * HALF, HALF)
        with jax.named_scope("last%d" % half):

            @pl.when(has_low)
            def _():
                part_arrival(0, p, half).wait_recv()
                partial[3, rows] += landed[0, p, rows].astype(F32)

            @pl.when(has_high)
            def _():
                part_arrival(1, p, half).wait_recv()
                partial[3, rows] += landed[1, p, rows].astype(F32)

            gradient_now = partial[3, rows] * FACTOR
            moment = BETA_FIRST * firsts[rows].astype(F32) + (1.0 - BETA_FIRST) * gradient_now
            spread = (
                BETA_SECOND * seconds[rows] + (1.0 - BETA_SECOND) * gradient_now * gradient_now
            )
            step = moment / (jnp.sqrt(spread) + EPSILON)
            partial[1, rows] = moment
            partial[2, rows] = partial[0, rows] - (MIXING * INNER_RATE) * step
            for slot, out in ((1, first_out), (2, merged_out)):
                store = pltpu.make_async_copy(
                    partial.at[slot, rows], out.at[rows], out_sem.at[LINE + 2 * half + slot - 1]
                )
                store.start()
                stores.append(store)

    with jax.named_scope("drain_back"):
        for i in range(LINE):
            for j in range(1, RING):
                back_copy(i, j).wait_recv()
    with jax.named_scope("drain"):
        for i in range(LINE):
            back_own(i).wait()
            for j in range(1, RING):
                back_copy(i, j).wait_send()
        for store in stores:
            store.wait()
        for copy in cot_copies + a_copies + b_copies + d_copies:
            copy.wait_send()
        for copies in act_copies:
            for copy in copies:
                copy.wait_send()
        for half in range(2):

            @pl.when(has_low)
            def _():
                w_copy(p, half, 1, p - 1).wait_send()

            @pl.when(has_high)
            def _():
                w_copy(p, half, 0, p + 1).wait_send()

            @pl.when(inner)
            def _():
                w_copy(p - 1, half, 0, p + 1).wait_send()
                w_copy(p + 1, half, 1, p - 1).wait_send()

            @pl.when(p == 1)
            def _():
                w_copy(3, half, 1, 0).wait_send()

            @pl.when(p == 2)
            def _():
                w_copy(0, half, 0, 3).wait_send()

            for k in range(LINE - 1):
                part_copy(k, half, 0, p).wait_send()


def on_device(activations, cotangent, params, first_moment, second_moment, anchor, outer_momentum):
    any_spec = pl.BlockSpec(memory_space=pl.ANY)
    dma = pltpu.SemaphoreType.DMA
    merged, first, grad = pl.pallas_call(
        kernel,
        out_shape=(
            jax.ShapeDtypeStruct((ROWS, KVW), F32),
            jax.ShapeDtypeStruct((ROWS, KVW), F32),
            jax.ShapeDtypeStruct((TOKENS, D), BF16),
        ),
        in_specs=[any_spec] * 7,
        out_specs=(any_spec,) * 3,
        scratch_shapes=[
            pltpu.VMEM((LINE, RING * TOKENS, ROWS), BF16),
            pltpu.VMEM((RING * TOKENS, KVW), BF16),
            pltpu.VMEM((LINE, ROWS, KVW), BF16),
            pltpu.VMEM((LINE, ROWS, KVW), F32),
            pltpu.VMEM((2, LINE, ROWS, KVW), BF16),
            pltpu.VMEM((LINE - 1, ROWS, KVW), BF16),
            pltpu.VMEM((LINE, RING * TOKENS, ROWS), BF16),
            pltpu.VMEM((ROWS, KVW), F32),
            pltpu.VMEM((ROWS, KVW), BF16),
            pltpu.VMEM((ROWS, KVW), F32),
            pltpu.VMEM((ROWS, KVW), BF16),
            pltpu.VMEM((ROWS, KVW), BF16),
            pltpu.VMEM((ROWS, KVW), BF16),
            pltpu.VMEM((CHIPS, CHUNK, KVW), BF16),
            pltpu.VMEM((CHUNK, KVW), F32),
            pltpu.VMEM((2, CHUNK, KVW), BF16),
            pltpu.VMEM((2, CHUNK, KVW), BF16),
            pltpu.VMEM((CHIPS, CHUNK, KVW), BF16),
            dma((10,)),
            dma((RING,)),
            dma((RING,)),
            dma((LINE, RING)),
            dma((LINE, RING)),
            dma((2, LINE, 2)),
            dma((LINE, 2)),
            dma((LINE - 1, 2)),
            dma((2, LINE, 2)),
            dma((LINE, RING)),
            dma((LINE, RING)),
            dma((CHIPS,)),
            dma((CHIPS,)),
            dma((2,)),
            dma((2,)),
            dma((CHIPS,)),
            dma((CHIPS,)),
            dma((2 * LINE,)),
        ],
        compiler_params=pltpu.CompilerParams(
            collective_id=0, has_side_effects=True, vmem_limit_bytes=56 * 2**20
        ),
        name="diloco_step",
    )(
        activations[0, 0],
        cotangent[0, 0],
        params[0],
        first_moment[0],
        second_moment[0],
        anchor,
        outer_momentum,
    )
    return merged[None], first[None], grad[None, None]


def solution(mesh):
    placed = (
        P("replica", None, "fsdp", None),
        P("replica", None, "fsdp", None),
        P("replica", "fsdp", None),
        P("replica", "fsdp", None),
        P("replica", "fsdp", None),
        P("fsdp", None),
        P("fsdp", None),
    )
    return jax.shard_map(
        on_device,
        mesh=mesh,
        in_specs=placed,
        out_specs=(
            P("replica", "fsdp", None),
            P("replica", "fsdp", None),
            P("replica", None, "fsdp", None),
        ),
        check_vma=False,
    )
```

time: 436 us -> 54 us (0.12)
  the two profiles are of different devices: /device:TPU:1 before, /device:TPU:6 now
where the time goes in v1:
time: 54 us; the launch traced here: 53.8 us
  Pallas kernels  49.4 us (91%)
  local copies, waits for them, and re-layouts  3.76 us (7%)
  between operations  0.66 us (1%)
    pallas_call x1, Pallas kernels, on_device(): pl.pallas_call(kernel, out_shape=(jax.ShapeDtypeStruct((ROWS, KVW), F32),...  49.4 us
    unnamed x7, local copies, waits for them, and re-layouts  3.76 us

profile of v1, /device:TPU:6, one launch (start us, length us, event | category | flops | bytes accessed | tf_op | source)
XLA Modules:
  0.0 53.8 jit_solution(8658170254389180143)
XLA Ops:
  0.6 49.4 %diloco_step.1 = (f32[256,512]{1,0:T(8,128)}, f32[256,512]{1,0:T(8,128)}, bf16[128,4096]{1,0:T(8,128)(2,1)}) custom-call(bf16[128,4096]{1,0:T(8,128)(2,1)} %bitcast.8, bf16[128,512]{1,0:T(8,128)(2,1)} %bitcast.15, f32[256,512]{1,0:T(8,128)} %bitcast.12, bf16[256,512]{1,0:T(8,128)(2,1)} %bitcast.14, f32[256,512]{1,0:T(8,128)} %bitcast.13, ...), custom_call_target="tpu_custom_call" | custom-call | tf_op jit(solution)/shard_map/diloco_step/pallas_call | solution.py:497
  50.1 0.0 copy-start.1
  50.1 0.0 copy-start
  50.1 2.0 %copy.13 = f32[1,256,512]{2,1,0:T(8,128)} copy(f32[1,256,512]{2,1,0:T(8,128)} %bitcast.11) | data formatting | bytes 1048576
  52.1 0.0 copy-done.1
  52.1 0.8 %copy.14 = f32[1,256,512]{2,1,0:T(8,128)} copy(f32[1,256,512]{2,1,0:T(8,128)S(1)} %bitcast.10) | data formatting | bytes 1048576
  52.9 0.0 copy-done
  52.9 1.0 %copy.15 = bf16[1,1,128,4096]{3,2,1,0:T(8,128)(2,1)} copy(bf16[1,1,128,4096]{3,2,1,0:T(8,128)(2,1)S(1)} %bitcast.9) | data formatting | bytes 2097152
Async XLA Ops:
  50.1 2.0 %copy-start.1 = (f32[256,512]{1,0:T(8,128)S(1)}, f32[256,512]{1,0:T(8,128)}, u32[]{:S(2)}) copy-start(f32[256,512]{1,0:T(8,128)} %get-tuple-element.7) | copy-start | bytes 1572868
  50.1 2.8 %copy-start = (bf16[128,4096]{1,0:T(8,128)(2,1)S(1)}, bf16[128,4096]{1,0:T(8,128)(2,1)}, u32[]{:S(2)}) copy-start(bf16[128,4096]{1,0:T(8,128)(2,1)} %get-tuple-element.8) | copy-start | bytes 3145732

commit v2 on v1

--- a/solution.py
+++ b/solution.py
@@ -13,6 +13,7 @@
 LINE = 4
 SPAN = ROWS * LINE
 HALF = ROWS // 2
+WIDE = KVW // 2
 CHIPS = 8
 CHUNK = ROWS // CHIPS
 REPLICAS = 32
@@ -55,12 +56,15 @@
     seconds,
     anchors,
     outers,
+    mixed,
     rounded,
     got_a,
     sum_a,
     sent_b,
     got_b,
     total,
+    near_sem,
+    far_sem,
     local_sem,
     cot_s,
     cot_r,
@@ -84,6 +88,7 @@
     shard = lax.axis_index("fsdp")
     y, p = shard // LINE, shard % LINE
     group, m = replica // CHIPS, replica % CHIPS
+    core = replica % 2
     edge = (p == 0) | (p == LINE - 1)
     inner = (p == 1) | (p == 2)
     has_low, has_high = p > 0, p < LINE - 1
@@ -126,6 +131,33 @@
 
     def features(ring_at, line_at):
         return pl.ds(pl.multiple_of(ring_at * SPAN + line_at * ROWS, ROWS), ROWS)
+
+    def columns(half):
+        return pl.ds(half * WIDE, WIDE)
+
+    barrier = pltpu.get_barrier_semaphore()
+
+    def signal(semaphore, where):
+        pl.semaphore_signal(semaphore, inc=1, device_id=where, device_id_type=MESH)
+
+    gate = replica - core
+    for j in range(1, RING):
+        signal(barrier, {"replica": gate, "fsdp": ring[j] * LINE + p})
+
+    @pl.when(has_low)
+    def _():
+        signal(barrier, {"replica": gate, "fsdp": shard - 1})
+
+    @pl.when(has_high)
+    def _():
+        signal(barrier, {"replica": gate, "fsdp": shard + 1})
+
+    for j in range(2, CHIPS, 2):
+        signal(barrier, {"replica": group * CHIPS + lax.rem(m - core + j, CHIPS)})
+
+    @pl.when(core == 1)
+    def _():
+        signal(barrier, {"replica": gate})
 
     own_rows = rows_of(y, TOKENS)
     loads = [
@@ -147,38 +179,46 @@
     for load in loads:
         load.start()
 
-    barrier = pltpu.get_barrier_semaphore()
-
-    def greet(where):
-        pl.semaphore_signal(barrier, inc=1, device_id=where, device_id_type=MESH)
-
-    for step in range(2):
-        greet(on_group(step))
-    for j in range(1, CHIPS):
-        greet(on_chip(j))
-    for j in range(1, RING):
-        greet(on_ring(j))
-
-    @pl.when(has_low)
-    def _():
-        greet(on_line(p - 1))
-
-    @pl.when(has_high)
-    def _():
-        greet(on_line(p + 1))
-
     with jax.named_scope("scale"):
         loads[0].wait()
         scaled[p] = (weights[...] * FACTOR).astype(BF16)
         rounded[...] = weights[...].astype(BF16)
 
-    with jax.named_scope("barrier"):
-        met = 2 + (CHIPS - 1) + (RING - 1)
-        pl.semaphore_wait(barrier, met + 2 - is_end)
+    with jax.named_scope("gate"):
+
+        @pl.when(core == 0)
+        def _():
+            pl.semaphore_wait(barrier, 2 * (RING - 1) + (CHIPS - 2) + 1 + 2 * (2 - is_end))
+            signal(near_sem, {"replica": gate + 1})
+
+        @pl.when(core == 1)
+        def _():
+            pl.semaphore_wait(near_sem, 1)
+            for step in range(2):
+                signal(barrier, on_group(step))
+
+    def await_far():
+        @pl.when(core == 1)
+        def _():
+            pl.semaphore_wait(barrier, 2)
+            signal(far_sem, {"replica": gate})
+
+        @pl.when(core == 0)
+        def _():
+            pl.semaphore_wait(far_sem, 1)
 
     cot_copies = [
-        remote(cot, cots.at[own_rows], cot_s.at[j], cot_r.at[j], on_ring(j))
-        for j in range(1, RING)
+        [
+            remote(
+                cot.at[:, columns(half)],
+                cots.at[own_rows, columns(half)],
+                cot_s.at[half, j],
+                cot_r.at[half, j],
+                on_ring(j),
+            )
+            for j in range(1, RING)
+        ]
+        for half in range(2)
     ]
     act_copies = [
         [
@@ -221,18 +261,17 @@
         return remote(rows, rows, w_s.at[way, block, half], w_r.at[block, half], on_line(to))
 
     def part_copy(k, half, way, to):
-        rows = pl.ds(half * HALF, HALF)
         return remote(
-            relay.at[k, rows],
-            landed.at[way, order[k], rows],
+            relay.at[k, half],
+            landed.at[way, order[k], half],
             part_s.at[k, half],
             part_r.at[way, order[k], half],
             on_line(to),
         )
 
     def part_arrival(way, block, half):
-        rows = landed.at[way, block, pl.ds(half * HALF, HALF)]
-        return remote(rows, rows, part_s.at[0, half], part_r.at[way, block, half], on_line(p))
+        piece = landed.at[way, block, half]
+        return remote(piece, piece, part_s.at[0, half], part_r.at[way, block, half], on_line(p))
 
     def back_copy(i, j):
         return remote(
@@ -248,8 +287,6 @@
             back.at[i, own_rows], grad_out.at[:, features(y, near[i])], out_sem.at[i]
         )
 
-    for copy in a_copies + cot_copies:
-        copy.start()
     for half in range(2):
 
         @pl.when(has_low)
@@ -260,7 +297,8 @@
         def _():
             w_copy(p, half, 0, p + 1).start()
 
-    for copies in act_copies:
+    in_turn = [cot_copies[0], act_copies[0], cot_copies[1], a_copies] + act_copies[1:]
+    for copies in in_turn:
         for copy in copies:
             copy.start()
 
@@ -290,61 +328,97 @@
                 w_copy(block, half, 0, p).wait_recv()
 
     def input_grad(i):
-        back[i] = lax.dot_general(
-            cots[...],
-            scaled[near[i]],
-            (((1,), (1,)), ((), ())),
+        with jax.named_scope("ig%d" % i):
+            if i > 0:
+                at_end_wait(near[i])
+            back[i] = lax.dot_general(
+                cots[...],
+                scaled[near[i]],
+                (((1,), (1,)), ((), ())),
+                preferred_element_type=F32,
+            ).astype(BF16)
+            for j in range(1, RING):
+                back_copy(i, j).start()
+            back_own(i).start()
+
+    def product(k, half):
+        partial[k, :, columns(half)] = lax.dot_general(
+            acts[k],
+            cots[:, columns(half)],
+            (((0,), (0,)), ((), ())),
             preferred_element_type=F32,
-        ).astype(BF16)
-        for j in range(1, RING):
-            back_copy(i, j).start()
-        back_own(i).start()
-
-    def gradient(k):
+        )
+        if k == LINE - 1:
+            return
+
+        @pl.when(edge)
+        def _():
+            relay[k, half] = partial[k, :, columns(half)].astype(BF16)
+
+        @pl.when(p == 0)
+        def _():
+            part_copy(k, half, 0, 1).start()
+
+        @pl.when(p == LINE - 1)
+        def _():
+            part_copy(k, half, 1, LINE - 2).start()
+
+    def act_wait(k):
         for copy in act_copies[k]:
             copy.wait_recv()
         loads[2 + k].wait()
-        with jax.named_scope("product"):
-            partial[k] = lax.dot_general(
-                acts[k], cots[...], (((0,), (0,)), ((), ())), preferred_element_type=F32
-            )
-        if k == LINE - 1:
+
+    def gradient(k):
+        with jax.named_scope("grad%d" % k):
+            act_wait(k)
+            product(k, 0)
+            product(k, 1)
+
+    def pass_part(k, half):
+        def onward(way, to):
+            part_arrival(way, order[k], half).wait_recv()
+            both = partial[k, :, columns(half)] + landed[way, order[k], half].astype(F32)
+            relay[k, half] = both.astype(BF16)
+            part_copy(k, half, way, to).start()
+
+        with jax.named_scope("part%d%d" % (k, half)):
+
+            @pl.when(inner & (order[k] > p))
+            def _():
+                onward(0, p + 1)
+
+            @pl.when(inner & (order[k] < p))
+            def _():
+                onward(1, p - 1)
+
+    def outer_step(step):
+        if step == 0:
+            await_far()
+            b_copies[0].start()
             return
-
-        @pl.when(edge)
-        def _():
-            relay[k] = partial[k].astype(BF16)
-
-        @pl.when(p == 0)
-        def _():
-            for half in range(2):
-                part_copy(k, half, 0, 1).start()
-
-        @pl.when(p == LINE - 1)
-        def _():
-            for half in range(2):
-                part_copy(k, half, 1, LINE - 2).start()
-
-    def pass_part(k, half):
-        rows = pl.ds(half * HALF, HALF)
-
-        @pl.when(inner)
-        def _():
-            goes_up = order[k] > p
-
-            @pl.when(goes_up)
-            def _():
-                part_arrival(0, order[k], half).wait_recv()
-                both = partial[k, rows] + landed[0, order[k], rows].astype(F32)
-                relay[k, rows] = both.astype(BF16)
-                part_copy(k, half, 0, p + 1).start()
-
-            @pl.when(order[k] < p)
-            def _():
-                part_arrival(1, order[k], half).wait_recv()
-                both = partial[k, rows] + landed[1, order[k], rows].astype(F32)
-                relay[k, rows] = both.astype(BF16)
-                part_copy(k, half, 1, p - 1).start()
+        b_copies[step - 1].wait_recv()
+        sum_a[...] += got_b[step - 1].astype(F32)
+        if step == 1:
+            sent_b[1] = sum_a[...].astype(BF16)
+            b_copies[1].start()
+            return
+        total[m] = sum_a[...].astype(BF16)
+        for copy in d_copies:
+            copy.start()
+
+    def outer_turn(turn):
+        with jax.named_scope("outer_turn%d" % turn):
+            if turn < 3:
+
+                @pl.when(group > 0)
+                def _():
+                    outer_step(turn)
+
+            if turn > 0:
+
+                @pl.when(group == 0)
+                def _():
+                    outer_step(turn - 1)
 
     with jax.named_scope("pass_near0"):
         pass_near(0)
@@ -355,98 +429,74 @@
             own_sum += got_a[j].astype(F32)
         sum_a[...] = own_sum
         sent_b[0] = own_sum.astype(BF16)
-        b_copies[0].start()
     with jax.named_scope("pass_near1"):
         pass_near(1)
-    with jax.named_scope("cot"):
+    outer_turn(0)
+    with jax.named_scope("grad00"):
         loads[1].wait()
-        for copy in cot_copies:
+        for copy in cot_copies[0]:
             copy.wait_recv()
-    with jax.named_scope("ig0"):
-        input_grad(0)
+        act_wait(0)
+        product(0, 0)
+    with jax.named_scope("grad01"):
+        for copy in cot_copies[1]:
+            copy.wait_recv()
+        product(0, 1)
     with jax.named_scope("pass_far0"):
         pass_far(0)
-    with jax.named_scope("grad0"):
-        gradient(0)
-    with jax.named_scope("sum_b0"):
-        b_copies[0].wait_recv()
-        sum_a[...] += got_b[0].astype(F32)
-        sent_b[1] = sum_a[...].astype(BF16)
-        b_copies[1].start()
+    outer_turn(1)
+    input_grad(0)
     with jax.named_scope("pass_far1"):
         pass_far(1)
-    with jax.named_scope("grad1"):
-        gradient(1)
-    with jax.named_scope("ig1"):
-        at_end_wait(near[1])
-        input_grad(1)
-    with jax.named_scope("part0"):
-        pass_part(0, 0)
-        pass_part(0, 1)
-    with jax.named_scope("grad2"):
-        gradient(2)
-    with jax.named_scope("sum_b1"):
-        b_copies[1].wait_recv()
-        sum_a[...] += got_b[1].astype(F32)
-        total[m] = sum_a[...].astype(BF16)
-        for copy in d_copies:
-            copy.start()
-    with jax.named_scope("ig2"):
-        at_end_wait(near[2])
-        input_grad(2)
-    with jax.named_scope("grad3"):
-        gradient(3)
-    with jax.named_scope("part1"):
-        pass_part(1, 0)
-        pass_part(1, 1)
-    with jax.named_scope("ig3"):
-        at_end_wait(near[3])
-        input_grad(3)
-    with jax.named_scope("part2"):
-        pass_part(2, 0)
-        pass_part(2, 1)
+    pass_part(0, 0)
+    gradient(1)
+    input_grad(1)
+    pass_part(0, 1)
+    gradient(2)
+    outer_turn(2)
+    input_grad(2)
+    pass_part(2, 0)
+    pass_part(1, 0)
+    gradient(3)
+    pass_part(2, 1)
+    input_grad(3)
+    pass_part(1, 1)
+    outer_turn(3)
     with jax.named_scope("outer"):
+        for load in loads[6:]:
+            load.wait()
         for j in range(1, CHIPS):
             d_arrival(j).wait_recv()
-        for load in loads[6:]:
-            load.wait()
         mean = total[...].astype(F32).reshape(ROWS, KVW) * (1.0 / REPLICAS)
         old = anchors[...].astype(F32)
         outer_grad = old - mean
         moment = OUTER_MOMENT * outers[...].astype(F32) + outer_grad
         new = old - OUTER_RATE * (outer_grad + OUTER_MOMENT * moment)
         kept = MIXING * (1.0 - INNER_RATE * WEIGHT_DECAY)
-        partial[0] = kept * weights[...] + (1.0 - MIXING) * new
-
-    stores = []
+        mixed[...] = kept * weights[...] + (1.0 - MIXING) * new
+
     for half in range(2):
-        rows = pl.ds(half * HALF, HALF)
+        cut = columns(half)
         with jax.named_scope("last%d" % half):
 
             @pl.when(has_low)
             def _():
                 part_arrival(0, p, half).wait_recv()
-                partial[3, rows] += landed[0, p, rows].astype(F32)
+                partial[3, :, cut] += landed[0, p, half].astype(F32)
 
             @pl.when(has_high)
             def _():
                 part_arrival(1, p, half).wait_recv()
-                partial[3, rows] += landed[1, p, rows].astype(F32)
-
-            gradient_now = partial[3, rows] * FACTOR
-            moment = BETA_FIRST * firsts[rows].astype(F32) + (1.0 - BETA_FIRST) * gradient_now
+                partial[3, :, cut] += landed[1, p, half].astype(F32)
+
+            gradient_now = partial[3, :, cut] * FACTOR
+            moment = BETA_FIRST * firsts[:, cut].astype(F32) + (1.0 - BETA_FIRST) * gradient_now
             spread = (
-                BETA_SECOND * seconds[rows] + (1.0 - BETA_SECOND) * gradient_now * gradient_now
+                BETA_SECOND * seconds[:, cut] + (1.0 - BETA_SECOND) * gradient_now * gradient_now
             )
             step = moment / (jnp.sqrt(spread) + EPSILON)
-            partial[1, rows] = moment
-            partial[2, rows] = partial[0, rows] - (MIXING * INNER_RATE) * step
-            for slot, out in ((1, first_out), (2, merged_out)):
-                store = pltpu.make_async_copy(
-                    partial.at[slot, rows], out.at[rows], out_sem.at[LINE + 2 * half + slot - 1]
-                )
-                store.start()
-                stores.append(store)
+            first_out[:, cut] = moment
+            merged_out[:, cut] = mixed[:, cut] - (MIXING * INNER_RATE) * step
 
     with jax.named_scope("drain_back"):
         for i in range(LINE):
@@ -457,11 +507,7 @@
             back_own(i).wait()
             for j in range(1, RING):
                 back_copy(i, j).wait_send()
-        for store in stores:
-            store.wait()
-        for copy in cot_copies + a_copies + b_copies + d_copies:
-            copy.wait_send()
-        for copies in act_copies:
+        for copies in in_turn + [b_copies, d_copies]:
             for copy in copies:
                 copy.wait_send()
         for half in range(2):
@@ -491,40 +537,57 @@
                 part_copy(k, half, 0, p).wait_send()
 
 
+def write_out(merged, first, grad, merged_out, first_out, grad_out, sem):
+    copies = [
+        pltpu.make_async_copy(merged, merged_out, sem.at[0]),
+        pltpu.make_async_copy(first, first_out, sem.at[1]),
+        pltpu.make_async_copy(grad, grad_out, sem.at[2]),
+    ]
+    for copy in copies:
+        copy.start()
+    for copy in copies:
+        copy.wait()
+
+
 def on_device(activations, cotangent, params, first_moment, second_moment, anchor, outer_momentum):
     any_spec = pl.BlockSpec(memory_space=pl.ANY)
+    vmem_spec = pl.BlockSpec(memory_space=pltpu.VMEM)
     dma = pltpu.SemaphoreType.DMA
-    merged, first, grad = pl.pallas_call(
+    results = (
+        jax.ShapeDtypeStruct((ROWS, KVW), F32),
+        jax.ShapeDtypeStruct((ROWS, KVW), F32),
+        jax.ShapeDtypeStruct((TOKENS, D), BF16),
+    )
+    held = pl.pallas_call(
         kernel,
-        out_shape=(
-            jax.ShapeDtypeStruct((ROWS, KVW), F32),
-            jax.ShapeDtypeStruct((ROWS, KVW), F32),
-            jax.ShapeDtypeStruct((TOKENS, D), BF16),
-        ),
+        out_shape=tuple(pltpu.VMEM(r.shape, r.dtype) for r in results),
         in_specs=[any_spec] * 7,
-        out_specs=(any_spec,) * 3,
+        out_specs=(vmem_spec,) * 3,
         scratch_shapes=[
             pltpu.VMEM((LINE, RING * TOKENS, ROWS), BF16),
             pltpu.VMEM((RING * TOKENS, KVW), BF16),
             pltpu.VMEM((LINE, ROWS, KVW), BF16),
             pltpu.VMEM((LINE, ROWS, KVW), F32),
-            pltpu.VMEM((2, LINE, ROWS, KVW), BF16),
-            pltpu.VMEM((LINE - 1, ROWS, KVW), BF16),
+            pltpu.VMEM((2, LINE, 2, ROWS, WIDE), BF16),
+            pltpu.VMEM((LINE - 1, 2, ROWS, WIDE), BF16),
             pltpu.VMEM((LINE, RING * TOKENS, ROWS), BF16),
             pltpu.VMEM((ROWS, KVW), F32),
             pltpu.VMEM((ROWS, KVW), BF16),
             pltpu.VMEM((ROWS, KVW), F32),
             pltpu.VMEM((ROWS, KVW), BF16),
             pltpu.VMEM((ROWS, KVW), BF16),
+            pltpu.VMEM((ROWS, KVW), F32),
             pltpu.VMEM((ROWS, KVW), BF16),
             pltpu.VMEM((CHIPS, CHUNK, KVW), BF16),
             pltpu.VMEM((CHUNK, KVW), F32),
             pltpu.VMEM((2, CHUNK, KVW), BF16),
             pltpu.VMEM((2, CHUNK, KVW), BF16),
             pltpu.VMEM((CHIPS, CHUNK, KVW), BF16),
+            pltpu.SemaphoreType.REGULAR,
+            pltpu.SemaphoreType.REGULAR,
             dma((10,)),
-            dma((RING,)),
-            dma((RING,)),
+            dma((2, RING)),
+            dma((2, RING)),
             dma((LINE, RING)),
             dma((LINE, RING)),
             dma((2, LINE, 2)),
@@ -539,10 +602,10 @@
             dma((2,)),
             dma((CHIPS,)),
             dma((CHIPS,)),
-            dma((2 * LINE,)),
+            dma((LINE,)),
         ],
         compiler_params=pltpu.CompilerParams(
-            collective_id=0, has_side_effects=True, vmem_limit_bytes=56 * 2**20
+            collective_id=0, has_side_effects=True, vmem_limit_bytes=58 * 2**20
         ),
         name="diloco_step",
     )(
@@ -554,6 +617,14 @@
         anchor,
         outer_momentum,
     )
+    merged, first, grad = pl.pallas_call(
+        write_out,
+        out_shape=results,
+        in_specs=[vmem_spec] * 3,
+        out_specs=(any_spec,) * 3,
+        scratch_shapes=[dma((3,))],
+        name="write_out",
+    )(*(pltpu.with_memory_space_constraint(x, pltpu.VMEM) for x in held))
     return merged[None], first[None], grad[None, None]
 
 

time: 54 us -> 44.9 us (0.83)
  the two profiles are of different devices: /device:TPU:6 before, /device:TPU:1 now
where the time goes in v2:
time: 44.9 us; the launch traced here: 44.3 us
  Pallas kernels  43.6 us (97%)
  between operations  0.64 us (1%)
    pallas_call x1, Pallas kernels, on_device(): pl.pallas_call(kernel, out_shape=tuple((pltpu.VMEM(r.shape, r.dtype) for...  42.3 us
    pallas_call x1, Pallas kernels, on_device(): pl.pallas_call(write_out, out_shape=results, in_specs=[vmem_spec] * 3, ou...  1.34 us

profile of v2, /device:TPU:1, one launch (start us, length us, event | category | flops | bytes accessed | tf_op | source)
XLA Modules:
  0.0 44.3 jit_solution(7476495226433122271)
XLA Ops:
  0.6 42.3 %diloco_step.1 = (f32[256,512]{1,0:T(8,128)S(1)}, f32[256,512]{1,0:T(8,128)S(1)}, bf16[128,4096]{1,0:T(8,128)(2,1)S(1)}) custom-call(bf16[128,4096]{1,0:T(8,128)(2,1)} %bitcast.8, bf16[128,512]{1,0:T(8,128)(2,1)} %bitcast.12, f32[256,512]{1,0:T(8,128)} %bitcast.9, bf16[256,512]{1,0:T(8,128)(2,1)} %bitcast.11, f32[256,512]{1,0:T(8,128)} %bitcast.10, ...), custom_call_target="tpu_custom_call" | custom-call | tf_op jit(solution)/shard_map/diloco_step/pallas_call | solution.py:561
  42.9 1.3 %write_out.1 = (f32[256,512]{1,0:T(8,128)}, f32[256,512]{1,0:T(8,128)}, bf16[128,4096]{1,0:T(8,128)(2,1)}) custom-call(f32[256,512]{1,0:T(8,128)S(1)} %get-tuple-element.9.merged, f32[256,512]{1,0:T(8,128)S(1)} %get-tuple-element.10.first, bf16[128,4096]{1,0:T(8,128)(2,1)S(1)} %get-tuple-element.11.grad), custom_call_target="tpu_custom_call" | custom-call | tf_op jit(solution)/shard_map/write_out/pallas_call | solution.py:620

commit v3 on v2

v3 whole, which is shorter than its diff:
```python
import jax
import jax.numpy as jnp
from jax import lax
from jax.experimental import pallas as pl
from jax.experimental.pallas import tpu as pltpu
from jax.sharding import PartitionSpec as P

D = 4096
KVW = 512
ROWS = 256
TOKENS = 128
RING = 4
LINE = 4
GROUPS = 4
SPAN = ROWS * LINE
HALF = ROWS // 2
WIDE = KVW // 2
CHIPS = 8
CHUNK = ROWS // CHIPS
REPLICAS = 32

BETA_FIRST = 0.9
BETA_SECOND = 0.95
EPSILON = 1e-08
WEIGHT_DECAY = 0.1
INNER_RATE = 0.03
OUTER_RATE = 0.7
OUTER_MOMENT = 0.9
MIXING = 0.5

FACTOR = float(D) ** (-0.5)
SWAPS_AT = (
    ((2, 0), (3, 0)),
    ((1, 0),),
    ((2, 1),),
    ((0, 0),),
    ((1, 1), (3, 1)),
    ((0, 1),),
    ((2, 2), (3, 2), (1, 2)),
    ((0, 2),),
)
MESH = pl.DeviceIdType.MESH
BF16 = jnp.bfloat16
F32 = jnp.float32


def kernel(
    act,
    cot,
    params,
    first,
    second,
    anchor,
    outer,
    merged_out,
    first_out,
    grad_out,
    acts,
    cots,
    scaled,
    partial,
    landed,
    relay,
    back,
    weights,
    state,
    seconds,
    mixed,
    rounded,
    got_a,
    sum_a,
    sent_b,
    got_b,
    total,
    near_sem,
    far_sem,
    local_sem,
    cot_s,
    cot_r,
    act_s,
    act_r,
    w_s,
    w_r,
    part_s,
    part_r,
    back_s,
    back_r,
    a_s,
    a_r,
    b_s,
    b_r,
    d_s,
    d_r,
    out_sem,
):
    replica = lax.axis_index("replica")
    shard = lax.axis_index("fsdp")
    y, p = shard // LINE, shard % LINE
    group, m = replica // CHIPS, replica % CHIPS
    core = replica % 2
    edge = (p == 0) | (p == LINE - 1)
    inner = (p == 1) | (p == 2)
    has_low, has_high = p > 0, p < LINE - 1
    upper = p // 2

    def mirrored(at):
        return at + upper * (LINE - 1 - 2 * at)

    is_end = 1 - (p + 1) % LINE // 2
    order = [mirrored(3), mirrored(2), mirrored(is_end), p]
    near = [p, mirrored(is_end), mirrored(2), mirrored(3)]
    ring = [lax.rem(y + j, RING) for j in range(RING)]
    chip = [lax.rem(m + j, CHIPS) for j in range(CHIPS)]
    swaps = [group + 1 - 2 * (group % 2), GROUPS - 1 - group]

    def on_ring(j):
        return {"fsdp": ring[j] * LINE + p}

    def on_line(at):
        return {"fsdp": y * LINE + at}

    def on_chip(j):
        return {"replica": group * CHIPS + chip[j]}

    def on_group(step):
        return {"replica": swaps[step] * CHIPS + m}

    def remote(src, dst, send, recv, where):
        return pltpu.make_async_remote_copy(
            src_ref=src,
            dst_ref=dst,
            send_sem=send,
            recv_sem=recv,
            device_id=where,
            device_id_type=MESH,
        )

    def rows_of(at, size):
        return pl.ds(pl.multiple_of(at * size, size), size)

    def features(ring_at, line_at):
        return pl.ds(pl.multiple_of(ring_at * SPAN + line_at * ROWS, ROWS), ROWS)

    def columns(half):
        return pl.ds(half * WIDE, WIDE)

    barrier = pltpu.get_barrier_semaphore()

    def signal(semaphore, where):
        pl.semaphore_signal(semaphore, inc=1, device_id=where, device_id_type=MESH)

    gate = replica - core + 1
    for j in range(1, RING):
        signal(barrier, {"replica": gate, "fsdp": ring[j] * LINE + p})

    @pl.when(has_low)
    def _():
        signal(barrier, {"replica": gate, "fsdp": shard - 1})

    @pl.when(has_high)
    def _():
        signal(barrier, {"replica": gate, "fsdp": shard + 1})

    for j in range(2, CHIPS, 2):
        signal(barrier, {"replica": group * CHIPS + lax.rem(m - core + j, CHIPS) + 1})

    @pl.when(core == 0)
    def _():
        signal(barrier, {"replica": gate})

    own_rows = rows_of(y, TOKENS)
    first_load = pltpu.make_async_copy(params, weights, local_sem.at[0])
    first_load.start()
    loads = [pltpu.make_async_copy(cot, cots.at[own_rows], local_sem.at[1])]
    for k in range(LINE):
        loads.append(
            pltpu.make_async_copy(
                act.at[:, features(y, order[k])], acts.at[k, own_rows], local_sem.at[2]
            )
        )
    loads += [
        pltpu.make_async_copy(anchor, state.at[0], local_sem.at[3]),
        pltpu.make_async_copy(outer, state.at[1], local_sem.at[3]),
        pltpu.make_async_copy(first, state.at[2], local_sem.at[3]),
        pltpu.make_async_copy(second, seconds, local_sem.at[4]),
    ]
    for load in loads:
        load.start()

    def await_bytes(like, semaphore):
        pltpu.make_async_copy(like, like, semaphore).wait()

    with jax.named_scope("scale"):
        first_load.wait()
        scaled[p] = (weights[...] * FACTOR).astype(BF16)
        rounded[...] = weights[...].astype(BF16)

    loads[0].wait()
    with jax.named_scope("gate"):

        @pl.when(core == 1)
        def _():
            pl.semaphore_wait(barrier, 2 * (RING - 1) + (CHIPS - 2) + 1 + 2 * (2 - is_end))
            signal(near_sem, {"replica": gate - 1})

        @pl.when(core == 0)
        def _():
            pl.semaphore_wait(near_sem, 1)
            for step in range(2):
                signal(barrier, on_group(step))

            @pl.when(group == 0)
            def _():
                signal(barrier, {"replica": 2 * CHIPS + m})

    def await_far():
        @pl.when(core == 0)
        def _():
            pl.semaphore_wait(barrier, 2 + jnp.where(group == 2, 1, 0))
            signal(far_sem, {"replica": gate})

        @pl.when(core == 1)
        def _():
            pl.semaphore_wait(far_sem, 1)

    def cot_copy(src, owner, half, slot, j):
        return remote(
            src, cots.at[rows_of(owner, TOKENS), columns(half)], cot_s, cot_r.at[slot], on_ring(j)
        )

    def cot_own(half, slot, j):
        return cot_copy(cots.at[own_rows, columns(half)], y, half, slot, j)

    def cot_passed(half, slot, j):
        owner = ring[RING - j]
        src = cots.at[rows_of(owner, TOKENS), columns(half)]
        return cot_copy(src, owner, half, slot, j)

    cot_copies = [
        cot_own(0, 0, 1),
        cot_own(1, 1, RING - 1),
        cot_own(1, 2, 1),
        cot_own(0, 3, RING - 1),
    ]
    cot_relays = [cot_passed(0, 4, 1), cot_passed(1, 5, RING - 1)]
    act_copies = [
        [
            remote(
                act.at[:, features(ring[j], order[k])],
                acts.at[k, own_rows],
                act_s,
                act_r.at[k],
                on_ring(j),
            )
            for j in range(1, RING)
        ]
        for k in range(LINE)
    ]
    a_copies = [
        remote(
            rounded.at[rows_of(chip[j], CHUNK)],
            got_a.at[j],
            a_s,
            a_r,
            on_chip(j),
        )
        for j in range(1, CHIPS)
    ]
    def b_copy(step, slot, to):
        where = {"replica": to * CHIPS + m}
        return remote(sent_b.at[step], got_b.at[slot], b_s, b_r.at[slot], where)

    d_copies = [
        remote(total.at[m], total.at[m], d_s, d_r, on_chip(j)) for j in range(1, CHIPS)
    ]

    def w_copy(block, half, way, to):
        rows = scaled.at[block, pl.ds(half * HALF, HALF)]
        return remote(rows, rows, w_s, w_r.at[block, half], on_line(to))

    def part_copy(k, half, way, to):
        slot = part_slot(way, order[k], to)
        return remote(
            relay.at[k, half], landed.at[slot, half], part_s, part_r.at[slot, half], on_line(to)
        )

    def part_slot(way, block, at):
        return jnp.where(block == at, LINE, block) if way == 1 else block

    def part_wait(way, block, half):
        slot = part_slot(way, block, p)
        await_bytes(landed.at[slot, half], part_r.at[slot, half])
        return landed[slot, half].astype(F32)

    def back_copy(i, j):
        return remote(
            back.at[i, rows_of(ring[j], TOKENS)],
            grad_out.at[:, features(y, near[i])],
            back_s,
            back_r,
            on_ring(j),
        )

    def back_own(i):
        return pltpu.make_async_copy(
            back.at[i, own_rows], grad_out.at[:, features(y, near[i])], out_sem
        )

    def w_start(half):
        @pl.when(has_low)
        def _():
            w_copy(p, half, 1, p - 1).start()

        @pl.when(has_high)
        def _():
            w_copy(p, half, 0, p + 1).start()

    for copy in a_copies:
        copy.start()
    for half in range(2):
        w_start(half)
    for copy in cot_copies + act_copies[0]:
        copy.start()

    def pass_near(half):
        @pl.when(inner)
        def _():
            w_copy(p - 1, half, 0, p + 1).wait_recv()
            w_copy(p - 1, half, 0, p + 1).start()
            w_copy(p + 1, half, 1, p - 1).wait_recv()
            w_copy(p + 1, half, 1, p - 1).start()

    def pass_far(half):
        @pl.when(p == 1)
        def _():
            w_copy(3, half, 1, 0).wait_recv()
            w_copy(3, half, 1, 0).start()

        @pl.when(p == 2)
        def _():
            w_copy(0, half, 0, 3).wait_recv()
            w_copy(0, half, 0, 3).start()

    def at_end_wait(block):
        @pl.when(edge)
        def _():
            for half in range(2):
                w_copy(block, half, 0, p).wait_recv()

    def input_grad(i):
        with jax.named_scope("ig%d" % i):
            if i > 0:
                at_end_wait(near[i])
            back[i] = lax.dot_general(
                cots[...],
                scaled[near[i]],
                (((1,), (1,)), ((), ())),
                preferred_element_type=F32,
            ).astype(BF16)
            for j in range(1, RING):
                back_copy(i, j).start()
            back_own(i).start()

    def product(k, half):
        partial[k, :, columns(half)] = lax.dot_general(
            acts[k],
            cots[:, columns(half)],
            (((0,), (0,)), ((), ())),
            preferred_element_type=F32,
        )
        if k == LINE - 1:
            return

        @pl.when(edge)
        def _():
            relay[k, half] = partial[k, :, columns(half)].astype(BF16)

        @pl.when(p == 0)
        def _():
            part_copy(k, half, 0, 1).start()

        @pl.when(p == LINE - 1)
        def _():
            part_copy(k, half, 1, LINE - 2).start()

    others = pl.ds(0, (RING - 1) * TOKENS)

    def cot_wait(slot):
        await_bytes(cots.at[pl.ds(0, TOKENS), columns(0)], cot_r.at[slot])

    def act_wait(k):
        await_bytes(acts.at[k, others], act_r.at[k])

    def gradient(k):
        with jax.named_scope("grad%d" % k):
            act_wait(k)
            product(k, 0)
            product(k, 1)

    def pass_part(k, half):
        def onward(way, to):
            both = partial[k, :, columns(half)] + part_wait(way, order[k], half)
            relay[k, half] = both.astype(BF16)
            part_copy(k, half, way, to).start()

        with jax.named_scope("part%d%d" % (k, half)):

            @pl.when(inner & (order[k] > p))
            def _():
                onward(0, p + 1)

            @pl.when(inner & (order[k] < p))
            def _():
                onward(1, p - 1)

    def outer_add(slot):
        b_copy(0, slot, swaps[0]).wait_recv()
        sum_a[...] += got_b[slot].astype(F32)

    def outer_step(step):
        if step == 0:
            await_far()
            b_copy(0, 0, swaps[0]).start()

            @pl.when(late)
            def _():
                b_copy(0, group - 1, 0).start()

        elif step == 1:
            outer_add(0)

            @pl.when(group < 3)
            def _():
                sent_b[1] = sum_a[...].astype(BF16)
                b_copy(1, 1, swaps[1]).start()

        else:

            @pl.when(group == 0)
            def _():
                outer_add(2)

            outer_add(1)
            total[m] = sum_a[...].astype(BF16)
            for copy in d_copies:
                copy.start()

    late = group > 1

    def outer_at(place):
        with jax.named_scope("outer_%d" % place):
            for member, step in SWAPS_AT[place]:

                @pl.when(group == member)
                def _():
                    outer_step(step)

    with jax.named_scope("cot_relay"):
        for slot in range(2):
            cot_wait(slot)
            cot_relays[slot].start()
    for copies in act_copies[1:]:
        for copy in copies:
            copy.start()
    with jax.named_scope("sum_a"):
        await_bytes(got_a.at[pl.ds(1, CHIPS - 1)], a_r)
        own_sum = weights[rows_of(m, CHUNK)]
        for j in range(1, CHIPS):
            own_sum += got_a[j].astype(F32)
        sum_a[...] = own_sum
        sent_b[0] = own_sum.astype(BF16)
    outer_at(0)
    with jax.named_scope("pass_near0"):
        pass_near(0)
    with jax.named_scope("pass_near1"):
        pass_near(1)
    outer_at(1)
    with jax.named_scope("grad00"):
        await_bytes(scaled.at[0], local_sem.at[2])
        cot_wait(3)
        cot_wait(4)
        act_wait(0)
        product(0, 0)
    with jax.named_scope("pass_far0"):
        pass_far(0)
    outer_at(2)
    with jax.named_scope("grad01"):
        cot_wait(2)
        cot_wait(5)
        product(0, 1)
    input_grad(0)
    outer_at(3)
    with jax.named_scope("pass_far1"):
        pass_far(1)
    pass_part(0, 0)
    input_grad(1)
    gradient(1)
    pass_part(0, 1)
    outer_at(4)
    gradient(2)
    input_grad(2)

    @pl.when(inner)
    def _():
        input_grad(3)

    outer_at(5)
    pass_part(2, 0)
    pass_part(1, 0)
    outer_at(6)
    gradient(3)
    pass_part(2, 1)
    pass_part(1, 1)
    outer_at(7)

    @pl.when(edge)
    def _():
        input_grad(3)

    with jax.named_scope("outer"):
        await_bytes(scaled.at[pl.ds(0, 3)], local_sem.at[3])
        loads[-1].wait()
        await_bytes(total.at[pl.ds(0, CHIPS - 1)], d_r)
        mean = total[...].astype(F32).reshape(ROWS, KVW) * (1.0 / REPLICAS)
        old = state[0].astype(F32)
        outer_grad = old - mean
        moment = OUTER_MOMENT * state[1].astype(F32) + outer_grad
        new = old - OUTER_RATE * (outer_grad + OUTER_MOMENT * moment)
        kept = MIXING * (1.0 - INNER_RATE * WEIGHT_DECAY)
        mixed[...] = kept * weights[...] + (1.0 - MIXING) * new

    for half in range(2):
        cut = columns(half)
        with jax.named_scope("last%d" % half):

            @pl.when(has_low)
            def _():
                partial[3, :, cut] += part_wait(0, p, half)

            @pl.when(has_high)
            def _():
                partial[3, :, cut] += part_wait(1, p, half)

            gradient_now = partial[3, :, cut] * FACTOR
            moment = BETA_FIRST * state[2, :, cut].astype(F32) + (1.0 - BETA_FIRST) * gradient_now
            spread = (
                BETA_SECOND * seconds[:, cut] + (1.0 - BETA_SECOND) * gradient_now * gradient_now
            )
            step = moment / (jnp.sqrt(spread) + EPSILON)
            first_out[:, cut] = moment
            merged_out[:, cut] = mixed[:, cut] - (MIXING * INNER_RATE) * step

    with jax.named_scope("drain_back"):
        three = landed.at[pl.ds(0, 3)]
        await_bytes(three, back_r)
    with jax.named_scope("drain"):
        await_bytes(scaled.at[0], out_sem)
        await_bytes(three, back_s)
        await_bytes(three, act_s)
        await_bytes(three, part_s)
        await_bytes(landed.at[pl.ds(0, 3), 0], cot_s)
        await_bytes(got_a.at[pl.ds(1, CHIPS - 1)], a_s)
        await_bytes(total.at[pl.ds(0, CHIPS - 1)], d_s)
        await_bytes(sent_b, b_s)

        @pl.when(group == 2)
        def _():
            await_bytes(sent_b.at[0], b_s)


        @pl.when(edge)
        def _():
            await_bytes(scaled.at[0], w_s)

        @pl.when(inner)
        def _():
            await_bytes(landed, w_s)


def write_out(merged, first, grad, merged_out, first_out, grad_out, sem):
    copies = [
        pltpu.make_async_copy(merged, merged_out, sem.at[0]),
        pltpu.make_async_copy(first, first_out, sem.at[1]),
        pltpu.make_async_copy(grad, grad_out, sem.at[2]),
    ]
    for copy in copies:
        copy.start()
    for copy in copies:
        copy.wait()


def on_device(activations, cotangent, params, first_moment, second_moment, anchor, outer_momentum):
    any_spec = pl.BlockSpec(memory_space=pl.ANY)
    vmem_spec = pl.BlockSpec(memory_space=pltpu.VMEM)
    dma = pltpu.SemaphoreType.DMA
    results = (
        jax.ShapeDtypeStruct((ROWS, KVW), F32),
        jax.ShapeDtypeStruct((ROWS, KVW), F32),
        jax.ShapeDtypeStruct((TOKENS, D), BF16),
    )
    held = pl.pallas_call(
        kernel,
        out_shape=tuple(pltpu.VMEM(r.shape, r.dtype) for r in results),
        in_specs=[any_spec] * 7,
        out_specs=(vmem_spec,) * 3,
        scratch_shapes=[
            pltpu.VMEM((LINE, RING * TOKENS, ROWS), BF16),
            pltpu.VMEM((RING * TOKENS, KVW), BF16),
            pltpu.VMEM((LINE, ROWS, KVW), BF16),
            pltpu.VMEM((LINE, ROWS, KVW), F32),
            pltpu.VMEM((LINE + 1, 2, ROWS, WIDE), BF16),
            pltpu.VMEM((LINE - 1, 2, ROWS, WIDE), BF16),
            pltpu.VMEM((LINE, RING * TOKENS, ROWS), BF16),
            pltpu.VMEM((ROWS, KVW), F32),
            pltpu.VMEM((3, ROWS, KVW), BF16),
            pltpu.VMEM((ROWS, KVW), F32),
            pltpu.VMEM((ROWS, KVW), F32),
            pltpu.VMEM((ROWS, KVW), BF16),
            pltpu.VMEM((CHIPS, CHUNK, KVW), BF16),
            pltpu.VMEM((CHUNK, KVW), F32),
            pltpu.VMEM((2, CHUNK, KVW), BF16),
            pltpu.VMEM((3, CHUNK, KVW), BF16),
            pltpu.VMEM((CHIPS, CHUNK, KVW), BF16),
            pltpu.SemaphoreType.REGULAR,
            pltpu.SemaphoreType.REGULAR,
            dma((5,)),
            dma,
            dma((6,)),
            dma,
            dma((LINE,)),
            dma,
            dma((LINE, 2)),
            dma,
            dma((LINE + 1, 2)),
            dma,
            dma,
            dma,
            dma,
            dma,
            dma((3,)),
            dma,
            dma,
            dma,
        ],
        compiler_params=pltpu.CompilerParams(
            collective_id=0, has_side_effects=True, vmem_limit_bytes=58 * 2**20
        ),
        name="diloco_step",
    )(
        activations[0, 0],
        cotangent[0, 0],
        params[0],
        first_moment[0],
        second_moment[0],
        anchor,
        outer_momentum,
    )
    merged, first, grad = pl.pallas_call(
        write_out,
        out_shape=results,
        in_specs=[vmem_spec] * 3,
        out_specs=(any_spec,) * 3,
        scratch_shapes=[dma((3,))],
        name="write_out",
    )(*(pltpu.with_memory_space_constraint(x, pltpu.VMEM) for x in held))
    return merged[None], first[None], grad[None, None]


def solution(mesh):
    placed = (
        P("replica", None, "fsdp", None),
        P("replica", None, "fsdp", None),
        P("replica", "fsdp", None),
        P("replica", "fsdp", None),
        P("replica", "fsdp", None),
        P("fsdp", None),
        P("fsdp", None),
    )
    return jax.shard_map(
        on_device,
        mesh=mesh,
        in_specs=placed,
        out_specs=(
            P("replica", "fsdp", None),
            P("replica", "fsdp", None),
            P("replica", None, "fsdp", None),
        ),
        check_vma=False,
    )
```

time: 44.9 us -> 41.9 us (0.933)
  the two profiles are of different devices: /device:TPU:1 before, /device:TPU:41 now
where the time goes in v3:
time: 41.9 us; the launch traced here: 41.8 us
  Pallas kernels  41.2 us (98%)
  between operations  0.64 us (2%)
    pallas_call x1, Pallas kernels, on_device(): pl.pallas_call(kernel, out_shape=tuple((pltpu.VMEM(r.shape, r.dtype) for...  39.8 us
    pallas_call x1, Pallas kernels, on_device(): pl.pallas_call(write_out, out_shape=results, in_specs=[vmem_spec] * 3, ou...  1.34 us

profile of v3, /device:TPU:41, one launch (start us, length us, event | category | flops | bytes accessed | tf_op | source)
XLA Modules:
  0.0 41.8 jit_solution(4853420918993078326)
XLA Ops:
  0.6 39.8 %diloco_step.1 = (f32[256,512]{1,0:T(8,128)S(1)}, f32[256,512]{1,0:T(8,128)S(1)}, bf16[128,4096]{1,0:T(8,128)(2,1)S(1)}) custom-call(bf16[128,4096]{1,0:T(8,128)(2,1)} %bitcast.8, bf16[128,512]{1,0:T(8,128)(2,1)} %bitcast.12, f32[256,512]{1,0:T(8,128)} %bitcast.9, bf16[256,512]{1,0:T(8,128)(2,1)} %bitcast.11, f32[256,512]{1,0:T(8,128)} %bitcast.10, ...), custom_call_target="tpu_custom_call" | custom-call | tf_op jit(solution)/shard_map/diloco_step/pallas_call | solution.py:601
  40.4 1.3 %write_out.1 = (f32[256,512]{1,0:T(8,128)}, f32[256,512]{1,0:T(8,128)}, bf16[128,4096]{1,0:T(8,128)(2,1)}) custom-call(f32[256,512]{1,0:T(8,128)S(1)} %get-tuple-element.9.merged, f32[256,512]{1,0:T(8,128)S(1)} %get-tuple-element.10.first, bf16[128,4096]{1,0:T(8,128)(2,1)S(1)} %get-tuple-element.11.grad), custom_call_target="tpu_custom_call" | custom-call | tf_op jit(solution)/shard_map/write_out/pallas_call | solution.py:658

commit v4 on v3

--- a/solution.py
+++ b/solution.py
@@ -18,6 +18,7 @@
 CHIPS = 8
 CHUNK = ROWS // CHIPS
 REPLICAS = 32
+PIECES = 1
 
 BETA_FIRST = 0.9
 BETA_SECOND = 0.95
@@ -29,15 +30,17 @@
 MIXING = 0.5
 
 FACTOR = float(D) ** (-0.5)
+ALL, ENDS, INSIDE, FOOT, ABOVE = range(5)
 SWAPS_AT = (
-    ((2, 0), (3, 0)),
-    ((1, 0),),
-    ((2, 1),),
-    ((0, 0),),
-    ((1, 1), (3, 1)),
-    ((0, 1),),
-    ((2, 2), (3, 2), (1, 2)),
-    ((0, 2),),
+    ((2, 0, ALL), (3, 0, ALL)),
+    ((1, 0, ALL),),
+    ((3, 1, FOOT),),
+    ((2, 1, ALL), (3, 1, ABOVE)),
+    ((0, 0, ALL),),
+    ((1, 1, ALL), (0, 1, ENDS)),
+    ((0, 1, INSIDE),),
+    ((2, 2, ALL), (3, 2, ALL), (1, 2, ALL)),
+    ((0, 2, ALL),),
 )
 MESH = pl.DeviceIdType.MESH
 BF16 = jnp.bfloat16
@@ -208,15 +211,10 @@
             pl.semaphore_wait(near_sem, 1)
             for step in range(2):
                 signal(barrier, on_group(step))
-
-            @pl.when(group == 0)
-            def _():
-                signal(barrier, {"replica": 2 * CHIPS + m})
-
     def await_far():
         @pl.when(core == 0)
         def _():
-            pl.semaphore_wait(barrier, 2 + jnp.where(group == 2, 1, 0))
+            pl.semaphore_wait(barrier, 2)
             signal(far_sem, {"replica": gate})
 
         @pl.when(core == 1)
@@ -243,19 +241,18 @@
         cot_own(0, 3, RING - 1),
     ]
     cot_relays = [cot_passed(0, 4, 1), cot_passed(1, 5, RING - 1)]
-    act_copies = [
-        [
-            remote(
-                act.at[:, features(ring[j], order[k])],
-                acts.at[k, own_rows],
-                act_s,
-                act_r.at[k],
-                on_ring(j),
-            )
-            for j in range(1, RING)
-        ]
-        for k in range(LINE)
-    ]
+    def act_copy(k, part, j):
+        if k == 0:
+            start = pl.multiple_of(ring[j] * SPAN + order[0] * ROWS + part * HALF, HALF)
+            src, dst = pl.ds(start, HALF), pl.ds(part * HALF, HALF)
+        else:
+            src, dst = features(ring[j], order[k]), pl.ds(0, ROWS)
+        return remote(
+            act.at[:, src], acts.at[k, own_rows, dst], act_s, act_r.at[k + part], on_ring(j)
+        )
+
+    act_parts = [(0, 0), (0, 1), (1, 1), (2, 1), (3, 1)]
+    act_copies = [[act_copy(k, part, j) for j in range(1, RING)] for k, part in act_parts]
     a_copies = [
         remote(
             rounded.at[rows_of(chip[j], CHUNK)],
@@ -361,10 +358,13 @@
                 back_copy(i, j).start()
             back_own(i).start()
 
+    def rows(half):
+        return pl.ds(half * HALF, HALF)
+
     def product(k, half):
-        partial[k, :, columns(half)] = lax.dot_general(
-            acts[k],
-            cots[:, columns(half)],
+        partial[k, rows(half)] = lax.dot_general(
+            acts[k, :, rows(half)],
+            cots[...],
             (((0,), (0,)), ((), ())),
             preferred_element_type=F32,
         )
@@ -373,7 +373,7 @@
 
         @pl.when(edge)
         def _():
-            relay[k, half] = partial[k, :, columns(half)].astype(BF16)
+            relay[k, half] = partial[k, rows(half)].astype(BF16)
 
         @pl.when(p == 0)
         def _():
@@ -388,8 +388,9 @@
     def cot_wait(slot):
         await_bytes(cots.at[pl.ds(0, TOKENS), columns(0)], cot_r.at[slot])
 
-    def act_wait(k):
-        await_bytes(acts.at[k, others], act_r.at[k])
+    def act_wait(k, part=1):
+        width = HALF if k == 0 else ROWS
+        await_bytes(acts.at[k, others, pl.ds(0, width)], act_r.at[k + part])
 
     def gradient(k):
         with jax.named_scope("grad%d" % k):
@@ -399,7 +400,7 @@
 
     def pass_part(k, half):
         def onward(way, to):
-            both = partial[k, :, columns(half)] + part_wait(way, order[k], half)
+            both = partial[k, rows(half)] + part_wait(way, order[k], half)
             relay[k, half] = both.astype(BF16)
             part_copy(k, half, way, to).start()
 
@@ -422,23 +423,12 @@
             await_far()
             b_copy(0, 0, swaps[0]).start()
 
-            @pl.when(late)
-            def _():
-                b_copy(0, group - 1, 0).start()
-
         elif step == 1:
             outer_add(0)
-
-            @pl.when(group < 3)
-            def _():
-                sent_b[1] = sum_a[...].astype(BF16)
-                b_copy(1, 1, swaps[1]).start()
+            sent_b[1] = sum_a[...].astype(BF16)
+            b_copy(1, 1, swaps[1]).start()
 
         else:
-
-            @pl.when(group == 0)
-            def _():
-                outer_add(2)
 
             outer_add(1)
             total[m] = sum_a[...].astype(BF16)
@@ -449,9 +439,9 @@
 
     def outer_at(place):
         with jax.named_scope("outer_%d" % place):
-            for member, step in SWAPS_AT[place]:
-
-                @pl.when(group == member)
+            for member, step, where in SWAPS_AT[place]:
+
+                @pl.when((group == member) & (True, edge, inner, p == 0, has_low)[where])
                 def _():
                     outer_step(step)
 
@@ -475,28 +465,28 @@
     with jax.named_scope("pass_near1"):
         pass_near(1)
     outer_at(1)
+    outer_at(2)
     with jax.named_scope("grad00"):
         await_bytes(scaled.at[0], local_sem.at[2])
-        cot_wait(3)
-        cot_wait(4)
-        act_wait(0)
+        for slot in range(2, 6):
+            cot_wait(slot)
+        act_wait(0, 0)
         product(0, 0)
+    with jax.named_scope("grad01"):
+        act_wait(0, 1)
+        product(0, 1)
+    outer_at(3)
     with jax.named_scope("pass_far0"):
         pass_far(0)
-    outer_at(2)
-    with jax.named_scope("grad01"):
-        cot_wait(2)
-        cot_wait(5)
-        product(0, 1)
     input_grad(0)
-    outer_at(3)
+    outer_at(4)
     with jax.named_scope("pass_far1"):
         pass_far(1)
     pass_part(0, 0)
     input_grad(1)
     gradient(1)
     pass_part(0, 1)
-    outer_at(4)
+    outer_at(5)
     gradient(2)
     input_grad(2)
 
@@ -504,14 +494,14 @@
     def _():
         input_grad(3)
 
-    outer_at(5)
+    outer_at(6)
     pass_part(2, 0)
     pass_part(1, 0)
-    outer_at(6)
+    outer_at(7)
     gradient(3)
     pass_part(2, 1)
+    outer_at(8)
     pass_part(1, 1)
-    outer_at(7)
 
     @pl.when(edge)
     def _():
@@ -530,25 +520,25 @@
         mixed[...] = kept * weights[...] + (1.0 - MIXING) * new
 
     for half in range(2):
-        cut = columns(half)
+        cut = rows(half)
         with jax.named_scope("last%d" % half):
 
             @pl.when(has_low)
             def _():
-                partial[3, :, cut] += part_wait(0, p, half)
+                partial[3, cut] += part_wait(0, p, half)
 
             @pl.when(has_high)
             def _():
-                partial[3, :, cut] += part_wait(1, p, half)
-
-            gradient_now = partial[3, :, cut] * FACTOR
-            moment = BETA_FIRST * state[2, :, cut].astype(F32) + (1.0 - BETA_FIRST) * gradient_now
+                partial[3, cut] += part_wait(1, p, half)
+
+            gradient_now = partial[3, cut] * FACTOR
+            moment = BETA_FIRST * state[2, cut].astype(F32) + (1.0 - BETA_FIRST) * gradient_now
             spread = (
-                BETA_SECOND * seconds[:, cut] + (1.0 - BETA_SECOND) * gradient_now * gradient_now
+                BETA_SECOND * seconds[cut] + (1.0 - BETA_SECOND) * gradient_now * gradient_now
             )
             step = moment / (jnp.sqrt(spread) + EPSILON)
-            first_out[:, cut] = moment
-            merged_out[:, cut] = mixed[:, cut] - (MIXING * INNER_RATE) * step
+            first_out[cut] = moment
+            merged_out[cut] = mixed[cut] - (MIXING * INNER_RATE) * step
 
     with jax.named_scope("drain_back"):
         three = landed.at[pl.ds(0, 3)]
@@ -563,11 +553,6 @@
         await_bytes(total.at[pl.ds(0, CHIPS - 1)], d_s)
         await_bytes(sent_b, b_s)
 
-        @pl.when(group == 2)
-        def _():
-            await_bytes(sent_b.at[0], b_s)
-
-
         @pl.when(edge)
         def _():
             await_bytes(scaled.at[0], w_s)
@@ -578,11 +563,12 @@
 
 
 def write_out(merged, first, grad, merged_out, first_out, grad_out, sem):
-    copies = [
-        pltpu.make_async_copy(merged, merged_out, sem.at[0]),
-        pltpu.make_async_copy(first, first_out, sem.at[1]),
-        pltpu.make_async_copy(grad, grad_out, sem.at[2]),
-    ]
+    copies = []
+    for src, dst in ((grad, grad_out), (merged, merged_out), (first, first_out)):
+        size = src.shape[0] // PIECES
+        for i in range(PIECES):
+            cut = pl.ds(i * size, size)
+            copies.append(pltpu.make_async_copy(src.at[cut], dst.at[cut], sem.at[len(copies)]))
     for copy in copies:
         copy.start()
     for copy in copies:
@@ -608,8 +594,8 @@
             pltpu.VMEM((RING * TOKENS, KVW), BF16),
             pltpu.VMEM((LINE, ROWS, KVW), BF16),
             pltpu.VMEM((LINE, ROWS, KVW), F32),
-            pltpu.VMEM((LINE + 1, 2, ROWS, WIDE), BF16),
-            pltpu.VMEM((LINE - 1, 2, ROWS, WIDE), BF16),
+            pltpu.VMEM((LINE + 1, 2, HALF, KVW), BF16),
+            pltpu.VMEM((LINE - 1, 2, HALF, KVW), BF16),
             pltpu.VMEM((LINE, RING * TOKENS, ROWS), BF16),
             pltpu.VMEM((ROWS, KVW), F32),
             pltpu.VMEM((3, ROWS, KVW), BF16),
@@ -627,7 +613,7 @@
             dma,
             dma((6,)),
             dma,
-            dma((LINE,)),
+            dma((LINE + 1,)),
             dma,
             dma((LINE, 2)),
             dma,
@@ -660,7 +646,7 @@
         out_shape=results,
         in_specs=[vmem_spec] * 3,
         out_specs=(any_spec,) * 3,
-        scratch_shapes=[dma((3,))],
+        scratch_shapes=[dma((3 * PIECES,))],
         name="write_out",
     )(*(pltpu.with_memory_space_constraint(x, pltpu.VMEM) for x in held))
     return merged[None], first[None], grad[None, None]

time: 41.9 us -> 40.4 us (0.964)
  the two profiles are of different devices: /device:TPU:41 before, /device:TPU:1 now
where the time goes in v4:
time: 40.4 us; the launch traced here: 40.2 us
  Pallas kernels  39.6 us (98%)
  between operations  0.64 us (2%)
    pallas_call x1, Pallas kernels, on_device(): pl.pallas_call(kernel, out_shape=tuple((pltpu.VMEM(r.shape, r.dtype) for...  38.3 us
    pallas_call x1, Pallas kernels, on_device(): pl.pallas_call(write_out, out_shape=results, in_specs=[vmem_spec] * 3, ou...  1.34 us

profile of v4, /device:TPU:1, one launch (start us, length us, event | category | flops | bytes accessed | tf_op | source)
XLA Modules:
  0.0 40.2 jit_solution(7459926885868666878)
XLA Ops:
  0.6 38.3 %diloco_step.1 = (f32[256,512]{1,0:T(8,128)S(1)}, f32[256,512]{1,0:T(8,128)S(1)}, bf16[128,4096]{1,0:T(8,128)(2,1)S(1)}) custom-call(bf16[128,4096]{1,0:T(8,128)(2,1)} %bitcast.8, bf16[128,512]{1,0:T(8,128)(2,1)} %bitcast.12, f32[256,512]{1,0:T(8,128)} %bitcast.9, bf16[256,512]{1,0:T(8,128)(2,1)} %bitcast.11, f32[256,512]{1,0:T(8,128)} %bitcast.10, ...), custom_call_target="tpu_custom_call" | custom-call | tf_op jit(solution)/shard_map/diloco_step/pallas_call | solution.py:587
  38.9 1.3 %write_out.1 = (f32[256,512]{1,0:T(8,128)}, f32[256,512]{1,0:T(8,128)}, bf16[128,4096]{1,0:T(8,128)(2,1)}) custom-call(f32[256,512]{1,0:T(8,128)S(1)} %get-tuple-element.9.merged, f32[256,512]{1,0:T(8,128)S(1)} %get-tuple-element.10.first, bf16[128,4096]{1,0:T(8,128)(2,1)S(1)} %get-tuple-element.11.grad), custom_call_target="tpu_custom_call" | custom-call | tf_op jit(solution)/shard_map/write_out/pallas_call | solution.py:644

commit v5 on v4

--- a/solution.py
+++ b/solution.py
@@ -30,17 +30,17 @@
 MIXING = 0.5
 
 FACTOR = float(D) ** (-0.5)
-ALL, ENDS, INSIDE, FOOT, ABOVE = range(5)
+ALL, ENDS, INSIDE, FOOT, ABOVE, CORE0, CORE1, INSIDE0, REST = range(9)
 SWAPS_AT = (
     ((2, 0, ALL), (3, 0, ALL)),
     ((1, 0, ALL),),
     ((3, 1, FOOT),),
     ((2, 1, ALL), (3, 1, ABOVE)),
-    ((0, 0, ALL),),
-    ((1, 1, ALL), (0, 1, ENDS)),
+    ((0, 0, CORE0),),
+    ((0, 0, CORE1), (1, 1, ALL), (0, 1, ENDS)),
     ((0, 1, INSIDE),),
-    ((2, 2, ALL), (3, 2, ALL), (1, 2, ALL)),
-    ((0, 2, ALL),),
+    ((2, 2, ALL), (3, 2, ALL), (1, 2, ALL), (0, 2, INSIDE0)),
+    ((0, 2, REST),),
 )
 MESH = pl.DeviceIdType.MESH
 BF16 = jnp.bfloat16
@@ -152,24 +152,28 @@
     def signal(semaphore, where):
         pl.semaphore_signal(semaphore, inc=1, device_id=where, device_id_type=MESH)
 
-    gate = replica - core + 1
+    apart = group == 0
+    hub = jnp.where(apart, 0, 1)
+    hub_here = replica - core + hub
+    sibling = {"replica": replica + 1 - 2 * core}
+    near_gate = jnp.where(apart, replica, hub_here)
     for j in range(1, RING):
-        signal(barrier, {"replica": gate, "fsdp": ring[j] * LINE + p})
+        signal(barrier, {"replica": near_gate, "fsdp": ring[j] * LINE + p})
 
     @pl.when(has_low)
     def _():
-        signal(barrier, {"replica": gate, "fsdp": shard - 1})
+        signal(barrier, {"replica": near_gate, "fsdp": shard - 1})
 
     @pl.when(has_high)
     def _():
-        signal(barrier, {"replica": gate, "fsdp": shard + 1})
+        signal(barrier, {"replica": near_gate, "fsdp": shard + 1})
 
     for j in range(2, CHIPS, 2):
-        signal(barrier, {"replica": group * CHIPS + lax.rem(m - core + j, CHIPS) + 1})
-
-    @pl.when(core == 0)
+        signal(barrier, {"replica": group * CHIPS + lax.rem(m - core + j, CHIPS) + hub})
+
+    @pl.when(core != hub)
     def _():
-        signal(barrier, {"replica": gate})
+        signal(barrier, sibling)
 
     own_rows = rows_of(y, TOKENS)
     first_load = pltpu.make_async_copy(params, weights, local_sem.at[0])
@@ -201,21 +205,46 @@
     loads[0].wait()
     with jax.named_scope("gate"):
 
-        @pl.when(core == 1)
-        def _():
-            pl.semaphore_wait(barrier, 2 * (RING - 1) + (CHIPS - 2) + 1 + 2 * (2 - is_end))
-            signal(near_sem, {"replica": gate - 1})
+        of_ring = (RING - 1) + (2 - is_end)
+        of_chips = (CHIPS - 2) + 1
+        met = jnp.where(apart, of_ring + (1 - core) * of_chips, 2 * of_ring + of_chips)
+
+        @pl.when(apart | (core == 1))
+        def _():
+            pl.semaphore_wait(barrier, met)
+
+        @pl.when(core == hub)
+        def _():
+            signal(near_sem, sibling)
+
+        @pl.when((core == 0) & (group > 0))
+        def _():
+            pl.semaphore_wait(near_sem, 1)
+
+        for step in range(2):
+
+            @pl.when((core == 0) & (swaps[step] > 0))
+            def _():
+                signal(barrier, on_group(step))
+
+    def await_far():
+        @pl.when((core == 0) & (group > 0))
+        def _():
+            pl.semaphore_wait(barrier, 2)
+
+        @pl.when((core == 0) & apart)
+        def _():
+            pl.semaphore_wait(far_sem, 2)
 
         @pl.when(core == 0)
         def _():
-            pl.semaphore_wait(near_sem, 1)
-            for step in range(2):
-                signal(barrier, on_group(step))
-    def await_far():
-        @pl.when(core == 0)
-        def _():
-            pl.semaphore_wait(barrier, 2)
-            signal(far_sem, {"replica": gate})
+            signal(far_sem, sibling)
+
+        for step in range(2):
+
+            @pl.when((core == 0) & (swaps[step] == 0))
+            def _():
+                signal(far_sem, on_group(step))
 
         @pl.when(core == 1)
         def _():
@@ -312,12 +341,24 @@
         def _():
             w_copy(p, half, 0, p + 1).start()
 
-    for copy in a_copies:
-        copy.start()
+    later = apart & (core == 1)
+
+    @pl.when(jnp.logical_not(later))
+    def _():
+        for copy in a_copies:
+            copy.start()
+
     for half in range(2):
         w_start(half)
     for copy in cot_copies + act_copies[0]:
         copy.start()
+
+    @pl.when(later)
+    def _():
+        pl.semaphore_wait(near_sem, 1)
+        for copy in a_copies:
+            copy.start()
+
 
     def pass_near(half):
         @pl.when(inner)
@@ -437,11 +478,15 @@
 
     late = group > 1
 
+    inside0 = inner & (core == 0)
+    spots = (True, edge, inner, p == 0, has_low, core == 0, core == 1, inside0)
+    spots += (jnp.logical_not(inside0),)
+
     def outer_at(place):
         with jax.named_scope("outer_%d" % place):
             for member, step, where in SWAPS_AT[place]:
 
-                @pl.when((group == member) & (True, edge, inner, p == 0, has_low)[where])
+                @pl.when((group == member) & spots[where])
                 def _():
                     outer_step(step)
 
@@ -462,9 +507,9 @@
     outer_at(0)
     with jax.named_scope("pass_near0"):
         pass_near(0)
+    outer_at(1)
     with jax.named_scope("pass_near1"):
         pass_near(1)
-    outer_at(1)
     outer_at(2)
     with jax.named_scope("grad00"):
         await_bytes(scaled.at[0], local_sem.at[2])
@@ -479,9 +524,9 @@
     with jax.named_scope("pass_far0"):
         pass_far(0)
     input_grad(0)
-    outer_at(4)
     with jax.named_scope("pass_far1"):
         pass_far(1)
+    outer_at(4)
     pass_part(0, 0)
     input_grad(1)
     gradient(1)

time: 40.4 us -> 39.1 us (0.968)
  the two profiles are of different devices: /device:TPU:1 before, /device:TPU:57 now
where the time goes in v5:
time: 39.1 us; the launch traced here: 38.9 us
  Pallas kernels  38.3 us (98%)
  between operations  0.64 us (2%)
    pallas_call x1, Pallas kernels, on_device(): pl.pallas_call(kernel, out_shape=tuple((pltpu.VMEM(r.shape, r.dtype) for...  37 us
    pallas_call x1, Pallas kernels, on_device(): pl.pallas_call(write_out, out_shape=results, in_specs=[vmem_spec] * 3, ou...  1.34 us

profile of v5, /device:TPU:57, one launch (start us, length us, event | category | flops | bytes accessed | tf_op | source)
XLA Modules:
  0.0 38.9 jit_solution(10321868533959106226)
XLA Ops:
  0.6 37.0 %diloco_step.1 = (f32[256,512]{1,0:T(8,128)S(1)}, f32[256,512]{1,0:T(8,128)S(1)}, bf16[128,4096]{1,0:T(8,128)(2,1)S(1)}) custom-call(bf16[128,4096]{1,0:T(8,128)(2,1)} %bitcast.8, bf16[128,512]{1,0:T(8,128)(2,1)} %bitcast.12, f32[256,512]{1,0:T(8,128)} %bitcast.9, bf16[256,512]{1,0:T(8,128)(2,1)} %bitcast.11, f32[256,512]{1,0:T(8,128)} %bitcast.10, ...), custom_call_target="tpu_custom_call" | custom-call | tf_op jit(solution)/shard_map/diloco_step/pallas_call | solution.py:632
  37.6 1.3 %write_out.1 = (f32[256,512]{1,0:T(8,128)}, f32[256,512]{1,0:T(8,128)}, bf16[128,4096]{1,0:T(8,128)(2,1)}) custom-call(f32[256,512]{1,0:T(8,128)S(1)} %get-tuple-element.9.merged, f32[256,512]{1,0:T(8,128)S(1)} %get-tuple-element.10.first, bf16[128,4096]{1,0:T(8,128)(2,1)S(1)} %get-tuple-element.11.grad), custom_call_target="tpu_custom_call" | custom-call | tf_op jit(solution)/shard_map/write_out/pallas_call | solution.py:689

commit v6 on v5

--- a/solution.py
+++ b/solution.py
@@ -552,17 +552,14 @@
     def _():
         input_grad(3)
 
-    with jax.named_scope("outer"):
+    of_mean = OUTER_RATE * (1.0 + OUTER_MOMENT)
+    with jax.named_scope("base"):
         await_bytes(scaled.at[pl.ds(0, 3)], local_sem.at[3])
         loads[-1].wait()
-        await_bytes(total.at[pl.ds(0, CHIPS - 1)], d_r)
-        mean = total[...].astype(F32).reshape(ROWS, KVW) * (1.0 / REPLICAS)
         old = state[0].astype(F32)
-        outer_grad = old - mean
-        moment = OUTER_MOMENT * state[1].astype(F32) + outer_grad
-        new = old - OUTER_RATE * (outer_grad + OUTER_MOMENT * moment)
+        known = (1.0 - of_mean) * old - OUTER_RATE * OUTER_MOMENT**2 * state[1].astype(F32)
         kept = MIXING * (1.0 - INNER_RATE * WEIGHT_DECAY)
-        mixed[...] = kept * weights[...] + (1.0 - MIXING) * new
+        mixed[...] = kept * weights[...] + (1.0 - MIXING) * known
 
     for half in range(2):
         cut = rows(half)
@@ -578,12 +575,15 @@
 
             gradient_now = partial[3, cut] * FACTOR
             moment = BETA_FIRST * state[2, cut].astype(F32) + (1.0 - BETA_FIRST) * gradient_now
-            spread = (
-                BETA_SECOND * seconds[cut] + (1.0 - BETA_SECOND) * gradient_now * gradient_now
-            )
+            spread = BETA_SECOND * seconds[cut] + (1.0 - BETA_SECOND) * gradient_now * gradient_now
             step = moment / (jnp.sqrt(spread) + EPSILON)
             first_out[cut] = moment
-            merged_out[cut] = mixed[cut] - (MIXING * INNER_RATE) * step
+            mixed[cut] -= (MIXING * INNER_RATE) * step
+
+    with jax.named_scope("outer"):
+        await_bytes(total.at[pl.ds(0, CHIPS - 1)], d_r)
+        share = (1.0 - MIXING) * of_mean / REPLICAS
+        merged_out[...] = mixed[...] + share * total[...].astype(F32).reshape(ROWS, KVW)
 
     with jax.named_scope("drain_back"):
         three = landed.at[pl.ds(0, 3)]

time: 39.1 us -> 38.6 us (0.987)
  the two profiles are of different devices: /device:TPU:57 before, /device:TPU:32 now
where the time goes in v6:
time: 38.6 us; the launch traced here: 38.4 us
  Pallas kernels  37.8 us (98%)
  between operations  0.64 us (2%)
    pallas_call x1, Pallas kernels, on_device(): pl.pallas_call(kernel, out_shape=tuple((pltpu.VMEM(r.shape, r.dtype) for...  36.5 us
    pallas_call x1, Pallas kernels, on_device(): pl.pallas_call(write_out, out_shape=results, in_specs=[vmem_spec] * 3, ou...  1.34 us

profile of v6, /device:TPU:32, one launch (start us, length us, event | category | flops | bytes accessed | tf_op | source)
XLA Modules:
  0.0 38.4 jit_solution(16976170716557912470)
XLA Ops:
  0.6 36.5 %diloco_step.1 = (f32[256,512]{1,0:T(8,128)S(1)}, f32[256,512]{1,0:T(8,128)S(1)}, bf16[128,4096]{1,0:T(8,128)(2,1)S(1)}) custom-call(bf16[128,4096]{1,0:T(8,128)(2,1)} %bitcast.8, bf16[128,512]{1,0:T(8,128)(2,1)} %bitcast.12, f32[256,512]{1,0:T(8,128)} %bitcast.9, bf16[256,512]{1,0:T(8,128)(2,1)} %bitcast.11, f32[256,512]{1,0:T(8,128)} %bitcast.10, ...), custom_call_target="tpu_custom_call" | custom-call | tf_op jit(solution)/shard_map/diloco_step/pallas_call | solution.py:632
  37.1 1.3 %write_out.1 = (f32[256,512]{1,0:T(8,128)}, f32[256,512]{1,0:T(8,128)}, bf16[128,4096]{1,0:T(8,128)(2,1)}) custom-call(f32[256,512]{1,0:T(8,128)S(1)} %get-tuple-element.9.merged, f32[256,512]{1,0:T(8,128)S(1)} %get-tuple-element.10.first, bf16[128,4096]{1,0:T(8,128)(2,1)S(1)} %get-tuple-element.11.grad), custom_call_target="tpu_custom_call" | custom-call | tf_op jit(solution)/shard_map/write_out/pallas_call | solution.py:689

commit v7 on v6

--- a/solution.py
+++ b/solution.py
@@ -343,6 +343,9 @@
 
     later = apart & (core == 1)
 
+    for copy in cot_copies:
+        copy.start()
+
     @pl.when(jnp.logical_not(later))
     def _():
         for copy in a_copies:
@@ -350,7 +353,7 @@
 
     for half in range(2):
         w_start(half)
-    for copy in cot_copies + act_copies[0]:
+    for copy in act_copies[0]:
         copy.start()
 
     @pl.when(later)

time: 38.6 us -> 38.6 us (level)
  no operation moved by 1% of the time
where the time goes in v7:
time: 38.6 us; the launch traced here: 38.4 us
  Pallas kernels  37.8 us (98%)
  between operations  0.64 us (2%)
    pallas_call x1, Pallas kernels, on_device(): pl.pallas_call(kernel, out_shape=tuple((pltpu.VMEM(r.shape, r.dtype) for...  36.5 us
    pallas_call x1, Pallas kernels, on_device(): pl.pallas_call(write_out, out_shape=results, in_specs=[vmem_spec] * 3, ou...  1.34 us

profile of v7, /device:TPU:32, one launch (start us, length us, event | category | flops | bytes accessed | tf_op | source)
XLA Modules:
  0.0 38.4 jit_solution(7526462124444374019)
XLA Ops:
  0.6 36.5 %diloco_step.1 = (f32[256,512]{1,0:T(8,128)S(1)}, f32[256,512]{1,0:T(8,128)S(1)}, bf16[128,4096]{1,0:T(8,128)(2,1)S(1)}) custom-call(bf16[128,4096]{1,0:T(8,128)(2,1)} %bitcast.8, bf16[128,512]{1,0:T(8,128)(2,1)} %bitcast.12, f32[256,512]{1,0:T(8,128)} %bitcast.9, bf16[256,512]{1,0:T(8,128)(2,1)} %bitcast.11, f32[256,512]{1,0:T(8,128)} %bitcast.10, ...), custom_call_target="tpu_custom_call" | custom-call | tf_op jit(solution)/shard_map/diloco_step/pallas_call | solution.py:635
  37.1 1.3 %write_out.1 = (f32[256,512]{1,0:T(8,128)}, f32[256,512]{1,0:T(8,128)}, bf16[128,4096]{1,0:T(8,128)(2,1)}) custom-call(f32[256,512]{1,0:T(8,128)S(1)} %get-tuple-element.9.merged, f32[256,512]{1,0:T(8,128)S(1)} %get-tuple-element.10.first, bf16[128,4096]{1,0:T(8,128)(2,1)S(1)} %get-tuple-element.11.grad), custom_call_target="tpu_custom_call" | custom-call | tf_op jit(solution)/shard_map/write_out/pallas_call | solution.py:692
